TPU v7x, 256 devices: a whole 4x4x8 slice. The times are simulated.
256 devices in a mesh: ctx: 16 (over y_lo, z), head: 4 (over x), req: 4 (over y_hi, core).
Axes of the slice: x: 4, y: 4 (y_hi: 2, y_lo: 2; y = y_hi * 2 + y_lo), z: 8, core: 2. Of those that a mesh axis runs over, the one named last changes fastest.
Arguments:
- queries: bfloat16 [4, 1024, 4096], P('req', 'ctx', 'head'), may hold values from -6 to 6
- keys: bfloat16 [4, 4096, 1024], P('req', 'ctx', 'head'), may hold values from -6 to 6
- values: bfloat16 [4, 4096, 1024], P('req', 'ctx', 'head'), may hold values from -6 to 6
- grad_out: bfloat16 [4, 1024, 4096], P('req', 'ctx', 'head'), may hold values from -6 to 6
- counts: int32 [4], P('req'), may hold values from 256 to 1024, as said below
- rate_table: float32 [16], replicated, may hold values from -2 to 0
- rate_index: int32 [4, 4096], P('req', 'ctx'), may hold values from 0 to 15
Outputs:
- grad_queries: bfloat16 [4, 1024, 4096], P('req', 'ctx', 'head')
- grad_keys: bfloat16 [4, 4096, 1024], P('req', 'ctx', 'head')
- grad_values: bfloat16 [4, 4096, 1024], P('req', 'ctx', 'head')
- grad_table: float32 [16], replicated
Inputs may be any that keep to these rules, and one draw needn't show every extreme that they name: `counts`: some request has exactly 1024 live candidates.
All inputs are finite; a program needn't handle non-finite values.
Results may differ from a plain program's by a relative error of at most 0.022.
Values may be sent and summed in bfloat16 or wider, within the bound.
A program may use at most 64 MiB of HBM per device.

v0:
```python
import jax
import jax.numpy as jnp
from jax import lax
from jax.sharding import PartitionSpec as P

HD = 128


score_scale = 128.0 ** (-0.5)


def passed_along(value, axis, by):
    size = lax.axis_size(axis)
    return lax.ppermute(value, axis, [(i, (i + by) % size) for i in range(size)])


def tile_scores(query_blk, key_blk, bias_blk):
    scores = jnp.einsum("cgjd,pgd->gjcp", query_blk, key_blk, preferred_element_type=jnp.float32)
    return scores * score_scale + bias_blk.astype(jnp.float32)


def stats_fold(carry, piece, query_blk):
    peak, total, accum = carry
    key_blk, value_blk, bias_blk = piece
    scores = tile_scores(query_blk, key_blk, bias_blk)
    new_peak = jnp.maximum(peak, jnp.max(scores, axis=-1))
    weights = jnp.exp(scores - new_peak[..., None])
    total = jnp.sum(weights, axis=-1)
    accum = jnp.einsum(
        "gjcp,pgd->gjcd", weights, value_blk.astype(jnp.float32), precision=lax.Precision.HIGHEST
    )
    return (new_peak, total, accum)


def tile_grads(query_blk, key_blk, value_blk, bias_blk, masked_blk, lse_blk, delta_blk):
    scores = tile_scores(query_blk, key_blk, bias_blk)
    prob = jnp.exp(scores - lse_blk[..., None])
    dprob = jnp.einsum("cgjd,pgd->gjcp", masked_blk, value_blk, preferred_element_type=jnp.float32)
    dscore = prob * (dprob - delta_blk[..., None])
    prob_b = prob.astype(jnp.bfloat16)
    dscore_b = dscore.astype(jnp.bfloat16)
    grad_v = jnp.einsum("gjcp,cgjd->pgd", prob_b, masked_blk, preferred_element_type=jnp.float32)
    grad_k = (
        jnp.einsum("gjcp,cgjd->pgd", dscore_b, query_blk, preferred_element_type=jnp.float32)
        * score_scale
    )
    grad_q = (
        jnp.einsum("gjcp,pgd->cgjd", dscore_b, key_blk, preferred_element_type=jnp.float32)
        * score_scale
    )
    column = jnp.sum(dscore, axis=(0, 1, 2))
    return (grad_q, grad_k, grad_v, column)


def shards(queries, keys, values, grad_out, counts, rate_table, rate_index):
    cycle_count = lax.axis_size("ctx")
    cycle_place = lax.axis_index("ctx")
    cand_dev = queries.shape[1]
    pre_dev = keys.shape[1]
    kv_dev = keys.shape[2] // HD
    group = queries.shape[2] // keys.shape[2]
    level_count = rate_table.shape[0]
    q_list, k_list, v_list = ([], [], [])
    slot_ids = cycle_place * cand_dev + jnp.arange(cand_dev, dtype=jnp.int32)
    level_ids = jnp.arange(level_count, dtype=jnp.int32)
    query_blk = queries[0].reshape(cand_dev, kv_dev, group, HD)
    key_blk = keys[0].reshape(pre_dev, kv_dev, HD)
    value_blk = values[0].reshape(pre_dev, kv_dev, HD)
    live = slot_ids < counts[0]
    masked_blk = jnp.where(live[:, None], grad_out[0], jnp.zeros_like(grad_out[0]))
    masked_blk = masked_blk.reshape(cand_dev, kv_dev, group, HD)
    one_hot = (rate_index[0][:, None] == level_ids[None, :]).astype(jnp.float32)
    bias_blk = jnp.dot(one_hot, rate_table, precision=lax.Precision.HIGHEST).astype(jnp.bfloat16)
    start_peak = jnp.full((kv_dev, group, cand_dev), -1e30, jnp.float32)
    start_total = jnp.zeros((kv_dev, group, cand_dev), jnp.float32)
    start_accum = jnp.zeros((kv_dev, group, cand_dev, HD), jnp.float32)
    fold_init = (start_peak, start_total, start_accum)
    folded = stats_fold(
        fold_init,
        (
            lax.all_gather(key_blk, "ctx", axis=0, tiled=True),
            lax.all_gather(value_blk, "ctx", axis=0, tiled=True),
            lax.all_gather(bias_blk, "ctx", axis=0, tiled=True),
        ),
        query_blk,
    )
    peak = folded[0]
    total = folded[1]
    accum = folded[2]
    lse_blk = peak + jnp.log(total)
    out_blk = accum / total[..., None]
    delta_blk = jnp.sum(
        jnp.transpose(masked_blk, (1, 2, 0, 3)).astype(jnp.float32) * out_blk, axis=-1
    )

    def key_step(step, carry):
        k_cur, v_cur, b_cur, dk_cur, dv_cur, db_cur, dq_acc = carry
        grad_q, grad_k, grad_v, column = tile_grads(
            query_blk, k_cur, v_cur, b_cur, masked_blk, lse_blk, delta_blk
        )
        dq_acc = dq_acc + grad_q
        dk_cur = dk_cur + grad_k
        dv_cur = dv_cur + grad_v
        db_cur = db_cur + column
        k_cur, v_cur, b_cur = passed_along((k_cur, v_cur, b_cur), "ctx", 1)
        dk_cur, dv_cur, db_cur = (
            passed_along(dk_cur.astype(jnp.bfloat16), "ctx", 1).astype(dk_cur.dtype),
            passed_along(dv_cur.astype(jnp.bfloat16), "ctx", 1).astype(dv_cur.dtype),
            passed_along(db_cur.astype(jnp.bfloat16), "ctx", 1).astype(db_cur.dtype),
        )
        return (k_cur, v_cur, b_cur, dk_cur, dv_cur, db_cur, dq_acc)

    start = (
        key_blk,
        value_blk,
        bias_blk,
        jnp.zeros((pre_dev, kv_dev, HD), jnp.float32),
        jnp.zeros((pre_dev, kv_dev, HD), jnp.float32),
        jnp.zeros((pre_dev,), jnp.float32),
        jnp.zeros((cand_dev, kv_dev, group, HD), jnp.float32),
    )
    final = lax.fori_loop(0, cycle_count, key_step, start)
    grad_k_all = final[3]
    grad_v_all = final[4]
    column_all = final[5]
    grad_q_all = final[6]
    q_list.append(grad_q_all.reshape(cand_dev, kv_dev * group * HD).astype(jnp.bfloat16))
    k_list.append(grad_k_all.reshape(pre_dev, kv_dev * HD).astype(jnp.bfloat16))
    v_list.append(grad_v_all.reshape(pre_dev, kv_dev * HD).astype(jnp.bfloat16))
    table_term = jnp.dot(column_all, one_hot, precision=lax.Precision.HIGHEST)
    grad_table = lax.psum(table_term, ("ctx", "head", "req"))
    return (jnp.stack(q_list), jnp.stack(k_list), jnp.stack(v_list), grad_table)


def solution(mesh):
    placed = (
        P("req", "ctx", "head"),
        P("req", "ctx", "head"),
        P("req", "ctx", "head"),
        P("req", "ctx", "head"),
        P("req"),
        P(),
        P("req", "ctx"),
    )
    return jax.shard_map(
        shards,
        mesh=mesh,
        in_specs=placed,
        out_specs=(P("req", "ctx", "head"), P("req", "ctx", "head"), P("req", "ctx", "head"), P()),
        check_vma=False,
    )
```

profile of v0, /device:TPU:1, one launch (start us, length us, event | category | flops | bytes accessed | tf_op | source)
XLA Modules:
  0.0 555.3 jit_solution(14008080075040852134)
XLA Ops:
  7.2 1.0 copy.26
  8.2 0.8 copy.32
  9.1 1.0 copy.27
  10.1 0.8 copy.33
  10.9 0.9 fusion.46
  11.9 30.9 %all-gather = bf16[16,1,256]{2,1,0:T(2,128)(2,1)S(1)} all-gather(bf16[1,1,256]{2,1,0:T(2,128)(2,1)S(1)} %reshape.65), channel_id=1, replica_groups=mesh['ctx'=16,'head'=4,'req'=4] {'ctx'}, dimensions={0}, use_global_device_ids=true | all-gather | bytes 8704 | tf_op jit(solution)/shard_map/all_gather | solution.py:83
  42.8 1.0 reshape_squeeze.11
  43.8 1.0 squeeze.7
  45.5 30.9 %all-gather.4.cloned.1.call-done = bf16[4096,2,128]{2,0,1:T(8,128)(2,1)} async-done(((bf16[256,2,128]{2,0,1:T(8,128)(2,1)}), bf16[4096,2,128]{2,0,1:T(8,128)(2,1)}) %all-gather.4.cloned.1.call-update) | async-done | bytes 2097168 | tf_op jit(solution)/shard_map/all_gather | solution.py:81
  76.5 2.9 bitcast_reduce_fusion
  79.4 3.2 copy-done.1
  82.6 1.9 fusion.24
  84.6 62.9 %all-gather.6.cloned.1.call-done = bf16[4096,2,128]{2,0,1:T(8,128)(2,1)} async-done(((bf16[256,2,128]{2,0,1:T(8,128)(2,1)}), bf16[4096,2,128]{2,0,1:T(8,128)(2,1)}) %all-gather.6.cloned.1.call-update) | async-done | bytes 2097168 | tf_op jit(solution)/shard_map/all_gather | solution.py:82
  147.5 9.1 %fusion.41 = f32[2,4,64]{2,1,0:T(4,128)S(1)} fusion(bf16[4096,2,128]{2,0,1:T(8,128)(2,1)} %all-gather.6.cloned.1.call-done, f32[2,4096,64,4]{1,2,3,0:T(8,128)} %copy-done.1, f32[2,4,64]{2,1,0:T(4,128)S(1)} %broadcast_maximum_fusion, f32[4096]{0:T(1024)S(1)} %bitcast.140, bf16[64,2,4,128]{3,0,2,1:T(8,128)(2,1)S(1)} %copy_select_fusion, ...), kind=kOutput, calls=%fused_computation.42 | convolution fusion | flops 3227778560 | bytes 10639360 | tf_op jit(solution)/shard_map/gjcp,pgd->gjcd/dot_general | solution.py:29
  156.7 270.3 %while.23 = (s32[]{:T(128)}, bf16[256,2,128]{2,0,1:T(8,128)(2,1)S(1)}, bf16[256,2,128]{2,0,1:T(8,128)(2,1)S(1)}, bf16[256]{0:T(256)(128)(2,1)S(1)}, f32[256,2,12...) while((s32[]{:T(128)}, ...), condition=%wide.region_5.6_spmd.clone, body=%wide.region_3.5_spmd.clone.sunk | while | flops 169608192 | bytes 8012674 | solution.py:122
  156.7 1.6 collective-permute-start
  159.5 2.1 collective-permute-start.5
  161.9 3.9 collective-permute-done.5
  166.1 5.6 %collective-permute-done.4 = bf16[256,2,128]{2,0,1:T(8,128)(2,1)S(1)} collective-permute-done((bf16[256,2,128]{2,0,1:T(8,128)(2,1)S(1)}, bf16[256,2,128]{2,0,1:T(8,128)(2,1)S(1)}, u32[]{:S(2)}, u32[]{:S(2)}) %collective-permute-start.4) | collective-permute-done | bytes 131104 | tf_op jit(solution)/shard_map/while/body/eval_jaxpr/ppermute | solution.py:14
  172.0 0.9 collective-permute-start.2
  173.7 3.5 collective-permute-start.3
  177.6 4.1 collective-permute-done.5
  181.7 0.9 collective-permute-start.4
  183.0 4.6 collective-permute-done.4
  188.9 1.7 collective-permute-start.3
  191.0 6.8 %collective-permute-done.5 = bf16[256]{0:T(256)(128)(2,1)S(1)} collective-permute-done((bf16[256]{0:T(256)(128)(2,1)S(1)}, bf16[256]{0:T(256)(128)(2,1)S(1)}, u32[]{:S(2)}, u32[]{:S(2)}) %collective-permute-start.5) | collective-permute-done | bytes 544 | tf_op jit(solution)/shard_map/while/body/eval_jaxpr/ppermute | solution.py:14
  198.2 5.6 %collective-permute-done.4 = bf16[256,2,128]{2,0,1:T(8,128)(2,1)S(1)} collective-permute-done((bf16[256,2,128]{2,0,1:T(8,128)(2,1)S(1)}, bf16[256,2,128]{2,0,1:T(8,128)(2,1)S(1)}, u32[]{:S(2)}, u32[]{:S(2)}) %collective-permute-start.4) | collective-permute-done | bytes 131104 | tf_op jit(solution)/shard_map/while/body/eval_jaxpr/ppermute | solution.py:14
  205.0 2.2 collective-permute-start.3
  207.6 8.5 %collective-permute-done.5 = bf16[256]{0:T(256)(128)(2,1)S(1)} collective-permute-done((bf16[256]{0:T(256)(128)(2,1)S(1)}, bf16[256]{0:T(256)(128)(2,1)S(1)}, u32[]{:S(2)}, u32[]{:S(2)}) %collective-permute-start.5) | collective-permute-done | bytes 544 | tf_op jit(solution)/shard_map/while/body/eval_jaxpr/ppermute | solution.py:14
  216.5 7.0 %collective-permute-done.4 = bf16[256,2,128]{2,0,1:T(8,128)(2,1)S(1)} collective-permute-done((bf16[256,2,128]{2,0,1:T(8,128)(2,1)S(1)}, bf16[256,2,128]{2,0,1:T(8,128)(2,1)S(1)}, u32[]{:S(2)}, u32[]{:S(2)}) %collective-permute-start.4) | collective-permute-done | bytes 131104 | tf_op jit(solution)/shard_map/while/body/eval_jaxpr/ppermute | solution.py:14
  225.9 9.8 %collective-permute-done.5 = bf16[256]{0:T(256)(128)(2,1)S(1)} collective-permute-done((bf16[256]{0:T(256)(128)(2,1)S(1)}, bf16[256]{0:T(256)(128)(2,1)S(1)}, u32[]{:S(2)}, u32[]{:S(2)}) %collective-permute-start.5) | collective-permute-done | bytes 544 | tf_op jit(solution)/shard_map/while/body/eval_jaxpr/ppermute | solution.py:14
  236.1 5.6 %collective-permute-done.4 = bf16[256,2,128]{2,0,1:T(8,128)(2,1)S(1)} collective-permute-done((bf16[256,2,128]{2,0,1:T(8,128)(2,1)S(1)}, bf16[256,2,128]{2,0,1:T(8,128)(2,1)S(1)}, u32[]{:S(2)}, u32[]{:S(2)}) %collective-permute-start.4) | collective-permute-done | bytes 131104 | tf_op jit(solution)/shard_map/while/body/eval_jaxpr/ppermute | solution.py:14
  243.4 8.4 %collective-permute-done.5 = bf16[256]{0:T(256)(128)(2,1)S(1)} collective-permute-done((bf16[256]{0:T(256)(128)(2,1)S(1)}, bf16[256]{0:T(256)(128)(2,1)S(1)}, u32[]{:S(2)}, u32[]{:S(2)}) %collective-permute-start.5) | collective-permute-done | bytes 544 | tf_op jit(solution)/shard_map/while/body/eval_jaxpr/ppermute | solution.py:14
  252.1 5.6 %collective-permute-done.4 = bf16[256,2,128]{2,0,1:T(8,128)(2,1)S(1)} collective-permute-done((bf16[256,2,128]{2,0,1:T(8,128)(2,1)S(1)}, bf16[256,2,128]{2,0,1:T(8,128)(2,1)S(1)}, u32[]{:S(2)}, u32[]{:S(2)}) %collective-permute-start.4) | collective-permute-done | bytes 131104 | tf_op jit(solution)/shard_map/while/body/eval_jaxpr/ppermute | solution.py:14
  259.0 1.1 collective-permute-start.3
  260.5 6.2 %collective-permute-done.5 = bf16[256]{0:T(256)(128)(2,1)S(1)} collective-permute-done((bf16[256]{0:T(256)(128)(2,1)S(1)}, bf16[256]{0:T(256)(128)(2,1)S(1)}, u32[]{:S(2)}, u32[]{:S(2)}) %collective-permute-start.5) | collective-permute-done | bytes 544 | tf_op jit(solution)/shard_map/while/body/eval_jaxpr/ppermute | solution.py:14
  267.0 6.4 %collective-permute-done.4 = bf16[256,2,128]{2,0,1:T(8,128)(2,1)S(1)} collective-permute-done((bf16[256,2,128]{2,0,1:T(8,128)(2,1)S(1)}, bf16[256,2,128]{2,0,1:T(8,128)(2,1)S(1)}, u32[]{:S(2)}, u32[]{:S(2)}) %collective-permute-start.4) | collective-permute-done | bytes 131104 | tf_op jit(solution)/shard_map/while/body/eval_jaxpr/ppermute | solution.py:14
  274.6 2.4 collective-permute-start.3
  277.4 6.3 %collective-permute-done.5 = bf16[256]{0:T(256)(128)(2,1)S(1)} collective-permute-done((bf16[256]{0:T(256)(128)(2,1)S(1)}, bf16[256]{0:T(256)(128)(2,1)S(1)}, u32[]{:S(2)}, u32[]{:S(2)}) %collective-permute-start.5) | collective-permute-done | bytes 544 | tf_op jit(solution)/shard_map/while/body/eval_jaxpr/ppermute | solution.py:14
  284.1 7.3 %collective-permute-done.4 = bf16[256,2,128]{2,0,1:T(8,128)(2,1)S(1)} collective-permute-done((bf16[256,2,128]{2,0,1:T(8,128)(2,1)S(1)}, bf16[256,2,128]{2,0,1:T(8,128)(2,1)S(1)}, u32[]{:S(2)}, u32[]{:S(2)}) %collective-permute-start.4) | collective-permute-done | bytes 131104 | tf_op jit(solution)/shard_map/while/body/eval_jaxpr/ppermute | solution.py:14
  292.7 0.8 collective-permute-start.3
  293.9 7.4 %collective-permute-done.5 = bf16[256]{0:T(256)(128)(2,1)S(1)} collective-permute-done((bf16[256]{0:T(256)(128)(2,1)S(1)}, bf16[256]{0:T(256)(128)(2,1)S(1)}, u32[]{:S(2)}, u32[]{:S(2)}) %collective-permute-start.5) | collective-permute-done | bytes 544 | tf_op jit(solution)/shard_map/while/body/eval_jaxpr/ppermute | solution.py:14
  301.6 5.6 %collective-permute-done.4 = bf16[256,2,128]{2,0,1:T(8,128)(2,1)S(1)} collective-permute-done((bf16[256,2,128]{2,0,1:T(8,128)(2,1)S(1)}, bf16[256,2,128]{2,0,1:T(8,128)(2,1)S(1)}, u32[]{:S(2)}, u32[]{:S(2)}) %collective-permute-start.4) | collective-permute-done | bytes 131104 | tf_op jit(solution)/shard_map/while/body/eval_jaxpr/ppermute | solution.py:14
  308.5 1.9 collective-permute-start.3
  310.9 5.3 collective-permute-done.5
  316.5 5.6 %collective-permute-done.4 = bf16[256,2,128]{2,0,1:T(8,128)(2,1)S(1)} collective-permute-done((bf16[256,2,128]{2,0,1:T(8,128)(2,1)S(1)}, bf16[256,2,128]{2,0,1:T(8,128)(2,1)S(1)}, u32[]{:S(2)}, u32[]{:S(2)}) %collective-permute-start.4) | collective-permute-done | bytes 131104 | tf_op jit(solution)/shard_map/while/body/eval_jaxpr/ppermute | solution.py:14
  323.4 1.9 collective-permute-start.3
  325.7 7.6 %collective-permute-done.5 = bf16[256]{0:T(256)(128)(2,1)S(1)} collective-permute-done((bf16[256]{0:T(256)(128)(2,1)S(1)}, bf16[256]{0:T(256)(128)(2,1)S(1)}, u32[]{:S(2)}, u32[]{:S(2)}) %collective-permute-start.5) | collective-permute-done | bytes 544 | tf_op jit(solution)/shard_map/while/body/eval_jaxpr/ppermute | solution.py:14
  333.6 6.0 %collective-permute-done.4 = bf16[256,2,128]{2,0,1:T(8,128)(2,1)S(1)} collective-permute-done((bf16[256,2,128]{2,0,1:T(8,128)(2,1)S(1)}, bf16[256,2,128]{2,0,1:T(8,128)(2,1)S(1)}, u32[]{:S(2)}, u32[]{:S(2)}) %collective-permute-start.4) | collective-permute-done | bytes 131104 | tf_op jit(solution)/shard_map/while/body/eval_jaxpr/ppermute | solution.py:14
  340.9 2.3 collective-permute-start.3
  343.6 9.2 %collective-permute-done.5 = bf16[256]{0:T(256)(128)(2,1)S(1)} collective-permute-done((bf16[256]{0:T(256)(128)(2,1)S(1)}, bf16[256]{0:T(256)(128)(2,1)S(1)}, u32[]{:S(2)}, u32[]{:S(2)}) %collective-permute-start.5) | collective-permute-done | bytes 544 | tf_op jit(solution)/shard_map/while/body/eval_jaxpr/ppermute | solution.py:14
  353.2 6.1 %collective-permute-done.4 = bf16[256,2,128]{2,0,1:T(8,128)(2,1)S(1)} collective-permute-done((bf16[256,2,128]{2,0,1:T(8,128)(2,1)S(1)}, bf16[256,2,128]{2,0,1:T(8,128)(2,1)S(1)}, u32[]{:S(2)}, u32[]{:S(2)}) %collective-permute-start.4) | collective-permute-done | bytes 131104 | tf_op jit(solution)/shard_map/while/body/eval_jaxpr/ppermute | solution.py:14
  361.1 9.6 %collective-permute-done.5 = bf16[256]{0:T(256)(128)(2,1)S(1)} collective-permute-done((bf16[256]{0:T(256)(128)(2,1)S(1)}, bf16[256]{0:T(256)(128)(2,1)S(1)}, u32[]{:S(2)}, u32[]{:S(2)}) %collective-permute-start.5) | collective-permute-done | bytes 544 | tf_op jit(solution)/shard_map/while/body/eval_jaxpr/ppermute | solution.py:14
  371.1 5.6 %collective-permute-done.4 = bf16[256,2,128]{2,0,1:T(8,128)(2,1)S(1)} collective-permute-done((bf16[256,2,128]{2,0,1:T(8,128)(2,1)S(1)}, bf16[256,2,128]{2,0,1:T(8,128)(2,1)S(1)}, u32[]{:S(2)}, u32[]{:S(2)}) %collective-permute-start.4) | collective-permute-done | bytes 131104 | tf_op jit(solution)/shard_map/while/body/eval_jaxpr/ppermute | solution.py:14
  378.4 7.5 %collective-permute-done.5 = bf16[256]{0:T(256)(128)(2,1)S(1)} collective-permute-done((bf16[256]{0:T(256)(128)(2,1)S(1)}, bf16[256]{0:T(256)(128)(2,1)S(1)}, u32[]{:S(2)}, u32[]{:S(2)}) %collective-permute-start.5) | collective-permute-done | bytes 544 | tf_op jit(solution)/shard_map/while/body/eval_jaxpr/ppermute | solution.py:14
  386.2 5.6 %collective-permute-done.4 = bf16[256,2,128]{2,0,1:T(8,128)(2,1)S(1)} collective-permute-done((bf16[256,2,128]{2,0,1:T(8,128)(2,1)S(1)}, bf16[256,2,128]{2,0,1:T(8,128)(2,1)S(1)}, u32[]{:S(2)}, u32[]{:S(2)}) %collective-permute-start.4) | collective-permute-done | bytes 131104 | tf_op jit(solution)/shard_map/while/body/eval_jaxpr/ppermute | solution.py:14
  393.1 2.0 collective-permute-start.3
  395.4 5.8 %collective-permute-done.5 = bf16[256]{0:T(256)(128)(2,1)S(1)} collective-permute-done((bf16[256]{0:T(256)(128)(2,1)S(1)}, bf16[256]{0:T(256)(128)(2,1)S(1)}, u32[]{:S(2)}, u32[]{:S(2)}) %collective-permute-start.5) | collective-permute-done | bytes 544 | tf_op jit(solution)/shard_map/while/body/eval_jaxpr/ppermute | solution.py:14
  401.6 7.3 %collective-permute-done.4 = bf16[256,2,128]{2,0,1:T(8,128)(2,1)S(1)} collective-permute-done((bf16[256,2,128]{2,0,1:T(8,128)(2,1)S(1)}, bf16[256,2,128]{2,0,1:T(8,128)(2,1)S(1)}, u32[]{:S(2)}, u32[]{:S(2)}) %collective-permute-start.4) | collective-permute-done | bytes 131104 | tf_op jit(solution)/shard_map/while/body/eval_jaxpr/ppermute | solution.py:14
  410.1 1.1 collective-permute-start.3
  411.6 7.7 %collective-permute-done.5 = bf16[256]{0:T(256)(128)(2,1)S(1)} collective-permute-done((bf16[256]{0:T(256)(128)(2,1)S(1)}, bf16[256]{0:T(256)(128)(2,1)S(1)}, u32[]{:S(2)}, u32[]{:S(2)}) %collective-permute-start.5) | collective-permute-done | bytes 544 | tf_op jit(solution)/shard_map/while/body/eval_jaxpr/ppermute | solution.py:14
  419.6 7.3 %collective-permute-done.4 = bf16[256,2,128]{2,0,1:T(8,128)(2,1)S(1)} collective-permute-done((bf16[256,2,128]{2,0,1:T(8,128)(2,1)S(1)}, bf16[256,2,128]{2,0,1:T(8,128)(2,1)S(1)}, u32[]{:S(2)}, u32[]{:S(2)}) %collective-permute-start.4) | collective-permute-done | bytes 131104 | tf_op jit(solution)/shard_map/while/body/eval_jaxpr/ppermute | solution.py:14
  429.1 0.8 convert_element_type.89
  429.9 118.5 %psum.7 = f32[16]{0:T(128)} all-reduce(f32[16]{0:T(128)S(1)} %convolution_bitcast_fusion.3), channel_id=1, replica_groups=mesh['ctx'=16,'head'=4,'req'=4] {'ctx','head','req'}, use_global_device_ids=true, to_apply=%region_6.7 | all-reduce | flops 16 | bytes 128 | tf_op jit(solution)/shard_map/psum | solution.py:131
  (387 shorter events, 33.3 us)
Async XLA Ops:
  7.2 69.3 %all-gather.4.cloned.1.call-start = ((), (), s32[]{:S(2)}) async-start(), calls=%async_computation | async-start | bytes 2228224 | tf_op jit(solution)/shard_map/all_gather | solution.py:81
  9.0 138.5 %all-gather.6.cloned.1.call-start = ((), (), s32[]{:S(2)}) async-start(), calls=%async_computation.1 | async-start | bytes 2228224 | tf_op jit(solution)/shard_map/all_gather | solution.py:82
  156.7 15.0 %collective-permute-start = (bf16[256,2,128]{2,0,1:T(8,128)(2,1)S(1)}, bf16[256,2,128]{2,0,1:T(8,128)(2,1)S(1)}, u32[]{:S(2)}, u32[]{:S(2)}) collective-permute-start(bf16[256,2,128]{2,0,1:T(8,128)(2,1)S(1)} %copy.58), channel_id=1, source_target_pairs={{0,16},{16,32},{32,48},{48,64},{64,80},{80,96},{96,112},{112,128},... | collective-permute-start | bytes 393224 | tf_op jit(solution)/shard_map/while/body/eval_jaxpr/ppermute | solution.py:14
  158.3 13.5 %collective-permute-start.1 = (bf16[256,2,128]{2,0,1:T(8,128)(2,1)S(1)}, bf16[256,2,128]{2,0,1:T(8,128)(2,1)S(1)}, u32[]{:S(2)}, u32[]{:S(2)}) collective-permute-start(bf16[256,2,128]{2,0,1:T(8,128)(2,1)S(1)} %copy.59), channel_id=1, source_target_pairs={{0,16},{16,32},{32,48},{48,64},{64,80},{80,96},{96,112},{112,128},... | collective-permute-start | bytes 393224 | tf_op jit(solution)/shard_map/while/body/eval_jaxpr/ppermute | solution.py:14
  158.4 13.3 %collective-permute-start.2 = (bf16[256]{0:T(256)(128)(2,1)S(1)}, bf16[256]{0:T(256)(128)(2,1)S(1)}, u32[]{:S(2)}, u32[]{:S(2)}) collective-permute-start(bf16[256]{0:T(256)(128)(2,1)S(1)} %copy.60), channel_id=1, source_target_pairs={{0,16},{16,32},{32,48},{48,64},{64,80},{80,96},{96,112},{112,128},... | collective-permute-start | bytes 1544 | tf_op jit(solution)/shard_map/while/body/eval_jaxpr/ppermute | solution.py:14
  171.8 15.9 %collective-permute-start = (bf16[256,2,128]{2,0,1:T(8,128)(2,1)S(1)}, bf16[256,2,128]{2,0,1:T(8,128)(2,1)S(1)}, u32[]{:S(2)}, u32[]{:S(2)}) collective-permute-start(bf16[256,2,128]{2,0,1:T(8,128)(2,1)S(1)} %copy.58), channel_id=1, source_target_pairs={{0,16},{16,32},{32,48},{48,64},{64,80},{80,96},{96,112},{112,128},... | collective-permute-start | bytes 393224 | tf_op jit(solution)/shard_map/while/body/eval_jaxpr/ppermute | solution.py:14
  171.9 15.8 %collective-permute-start.1 = (bf16[256,2,128]{2,0,1:T(8,128)(2,1)S(1)}, bf16[256,2,128]{2,0,1:T(8,128)(2,1)S(1)}, u32[]{:S(2)}, u32[]{:S(2)}) collective-permute-start(bf16[256,2,128]{2,0,1:T(8,128)(2,1)S(1)} %copy.59), channel_id=1, source_target_pairs={{0,16},{16,32},{32,48},{48,64},{64,80},{80,96},{96,112},{112,128},... | collective-permute-start | bytes 393224 | tf_op jit(solution)/shard_map/while/body/eval_jaxpr/ppermute | solution.py:14
  172.0 15.7 %collective-permute-start.2 = (bf16[256]{0:T(256)(128)(2,1)S(1)}, bf16[256]{0:T(256)(128)(2,1)S(1)}, u32[]{:S(2)}, u32[]{:S(2)}) collective-permute-start(bf16[256]{0:T(256)(128)(2,1)S(1)} %copy.60), channel_id=1, source_target_pairs={{0,16},{16,32},{32,48},{48,64},{64,80},{80,96},{96,112},{112,128},... | collective-permute-start | bytes 1544 | tf_op jit(solution)/shard_map/while/body/eval_jaxpr/ppermute | solution.py:14
  173.7 9.3 %collective-permute-start.3 = (bf16[256,2,128]{2,0,1:T(8,128)(2,1)S(1)}, bf16[256,2,128]{2,0,1:T(8,128)(2,1)S(1)}, u32[]{:S(2)}, u32[]{:S(2)}) collective-permute-start(bf16[256,2,128]{2,0,1:T(8,128)(2,1)S(1)} %fusion.86), channel_id=1, source_target_pairs={{0,16},{16,32},{32,48},{48,64},{64,80},{80,96},{96,112},{112,128},... | collective-permute-start | bytes 393224 | tf_op jit(solution)/shard_map/while/body/eval_jaxpr/ppermute | solution.py:14
  187.7 16.1 %collective-permute-start = (bf16[256,2,128]{2,0,1:T(8,128)(2,1)S(1)}, bf16[256,2,128]{2,0,1:T(8,128)(2,1)S(1)}, u32[]{:S(2)}, u32[]{:S(2)}) collective-permute-start(bf16[256,2,128]{2,0,1:T(8,128)(2,1)S(1)} %copy.58), channel_id=1, source_target_pairs={{0,16},{16,32},{32,48},{48,64},{64,80},{80,96},{96,112},{112,128},... | collective-permute-start | bytes 393224 | tf_op jit(solution)/shard_map/while/body/eval_jaxpr/ppermute | solution.py:14
  187.9 16.0 %collective-permute-start.1 = (bf16[256,2,128]{2,0,1:T(8,128)(2,1)S(1)}, bf16[256,2,128]{2,0,1:T(8,128)(2,1)S(1)}, u32[]{:S(2)}, u32[]{:S(2)}) collective-permute-start(bf16[256,2,128]{2,0,1:T(8,128)(2,1)S(1)} %copy.59), channel_id=1, source_target_pairs={{0,16},{16,32},{32,48},{48,64},{64,80},{80,96},{96,112},{112,128},... | collective-permute-start | bytes 393224 | tf_op jit(solution)/shard_map/while/body/eval_jaxpr/ppermute | solution.py:14
  188.0 15.8 %collective-permute-start.2 = (bf16[256]{0:T(256)(128)(2,1)S(1)}, bf16[256]{0:T(256)(128)(2,1)S(1)}, u32[]{:S(2)}, u32[]{:S(2)}) collective-permute-start(bf16[256]{0:T(256)(128)(2,1)S(1)} %copy.60), channel_id=1, source_target_pairs={{0,16},{16,32},{32,48},{48,64},{64,80},{80,96},{96,112},{112,128},... | collective-permute-start | bytes 1544 | tf_op jit(solution)/shard_map/while/body/eval_jaxpr/ppermute | solution.py:14
  188.9 9.2 %collective-permute-start.3 = (bf16[256,2,128]{2,0,1:T(8,128)(2,1)S(1)}, bf16[256,2,128]{2,0,1:T(8,128)(2,1)S(1)}, u32[]{:S(2)}, u32[]{:S(2)}) collective-permute-start(bf16[256,2,128]{2,0,1:T(8,128)(2,1)S(1)} %fusion.86), channel_id=1, source_target_pairs={{0,16},{16,32},{32,48},{48,64},{64,80},{80,96},{96,112},{112,128},... | collective-permute-start | bytes 393224 | tf_op jit(solution)/shard_map/while/body/eval_jaxpr/ppermute | solution.py:14
  203.9 19.7 %collective-permute-start = (bf16[256,2,128]{2,0,1:T(8,128)(2,1)S(1)}, bf16[256,2,128]{2,0,1:T(8,128)(2,1)S(1)}, u32[]{:S(2)}, u32[]{:S(2)}) collective-permute-start(bf16[256,2,128]{2,0,1:T(8,128)(2,1)S(1)} %copy.58), channel_id=1, source_target_pairs={{0,16},{16,32},{32,48},{48,64},{64,80},{80,96},{96,112},{112,128},... | collective-permute-start | bytes 393224 | tf_op jit(solution)/shard_map/while/body/eval_jaxpr/ppermute | solution.py:14
  204.0 19.6 %collective-permute-start.1 = (bf16[256,2,128]{2,0,1:T(8,128)(2,1)S(1)}, bf16[256,2,128]{2,0,1:T(8,128)(2,1)S(1)}, u32[]{:S(2)}, u32[]{:S(2)}) collective-permute-start(bf16[256,2,128]{2,0,1:T(8,128)(2,1)S(1)} %copy.59), channel_id=1, source_target_pairs={{0,16},{16,32},{32,48},{48,64},{64,80},{80,96},{96,112},{112,128},... | collective-permute-start | bytes 393224 | tf_op jit(solution)/shard_map/while/body/eval_jaxpr/ppermute | solution.py:14
  204.1 19.5 %collective-permute-start.2 = (bf16[256]{0:T(256)(128)(2,1)S(1)}, bf16[256]{0:T(256)(128)(2,1)S(1)}, u32[]{:S(2)}, u32[]{:S(2)}) collective-permute-start(bf16[256]{0:T(256)(128)(2,1)S(1)} %copy.60), channel_id=1, source_target_pairs={{0,16},{16,32},{32,48},{48,64},{64,80},{80,96},{96,112},{112,128},... | collective-permute-start | bytes 1544 | tf_op jit(solution)/shard_map/while/body/eval_jaxpr/ppermute | solution.py:14
  205.0 11.5 %collective-permute-start.3 = (bf16[256,2,128]{2,0,1:T(8,128)(2,1)S(1)}, bf16[256,2,128]{2,0,1:T(8,128)(2,1)S(1)}, u32[]{:S(2)}, u32[]{:S(2)}) collective-permute-start(bf16[256,2,128]{2,0,1:T(8,128)(2,1)S(1)} %fusion.86), channel_id=1, source_target_pairs={{0,16},{16,32},{32,48},{48,64},{64,80},{80,96},{96,112},{112,128},... | collective-permute-start | bytes 393224 | tf_op jit(solution)/shard_map/while/body/eval_jaxpr/ppermute | solution.py:14
  207.2 8.9 %collective-permute-start.5 = (bf16[256]{0:T(256)(128)(2,1)S(1)}, bf16[256]{0:T(256)(128)(2,1)S(1)}, u32[]{:S(2)}, u32[]{:S(2)}) collective-permute-start(bf16[256]{0:T(256)(128)(2,1)S(1)} %fusion.88), channel_id=1, source_target_pairs={{0,16},{16,32},{32,48},{48,64},{64,80},{80,96},{96,112},{112,128},... | collective-permute-start | bytes 1544 | tf_op jit(solution)/shard_map/while/body/eval_jaxpr/ppermute | solution.py:14
  223.6 18.1 %collective-permute-start = (bf16[256,2,128]{2,0,1:T(8,128)(2,1)S(1)}, bf16[256,2,128]{2,0,1:T(8,128)(2,1)S(1)}, u32[]{:S(2)}, u32[]{:S(2)}) collective-permute-start(bf16[256,2,128]{2,0,1:T(8,128)(2,1)S(1)} %copy.58), channel_id=1, source_target_pairs={{0,16},{16,32},{32,48},{48,64},{64,80},{80,96},{96,112},{112,128},... | collective-permute-start | bytes 393224 | tf_op jit(solution)/shard_map/while/body/eval_jaxpr/ppermute | solution.py:14
  223.7 18.0 %collective-permute-start.1 = (bf16[256,2,128]{2,0,1:T(8,128)(2,1)S(1)}, bf16[256,2,128]{2,0,1:T(8,128)(2,1)S(1)}, u32[]{:S(2)}, u32[]{:S(2)}) collective-permute-start(bf16[256,2,128]{2,0,1:T(8,128)(2,1)S(1)} %copy.59), channel_id=1, source_target_pairs={{0,16},{16,32},{32,48},{48,64},{64,80},{80,96},{96,112},{112,128},... | collective-permute-start | bytes 393224 | tf_op jit(solution)/shard_map/while/body/eval_jaxpr/ppermute | solution.py:14
  223.8 17.9 %collective-permute-start.2 = (bf16[256]{0:T(256)(128)(2,1)S(1)}, bf16[256]{0:T(256)(128)(2,1)S(1)}, u32[]{:S(2)}, u32[]{:S(2)}) collective-permute-start(bf16[256]{0:T(256)(128)(2,1)S(1)} %copy.60), channel_id=1, source_target_pairs={{0,16},{16,32},{32,48},{48,64},{64,80},{80,96},{96,112},{112,128},... | collective-permute-start | bytes 1544 | tf_op jit(solution)/shard_map/while/body/eval_jaxpr/ppermute | solution.py:14
  224.7 11.3 %collective-permute-start.3 = (bf16[256,2,128]{2,0,1:T(8,128)(2,1)S(1)}, bf16[256,2,128]{2,0,1:T(8,128)(2,1)S(1)}, u32[]{:S(2)}, u32[]{:S(2)}) collective-permute-start(bf16[256,2,128]{2,0,1:T(8,128)(2,1)S(1)} %fusion.86), channel_id=1, source_target_pairs={{0,16},{16,32},{32,48},{48,64},{64,80},{80,96},{96,112},{112,128},... | collective-permute-start | bytes 393224 | tf_op jit(solution)/shard_map/while/body/eval_jaxpr/ppermute | solution.py:14
  225.5 10.2 %collective-permute-start.5 = (bf16[256]{0:T(256)(128)(2,1)S(1)}, bf16[256]{0:T(256)(128)(2,1)S(1)}, u32[]{:S(2)}, u32[]{:S(2)}) collective-permute-start(bf16[256]{0:T(256)(128)(2,1)S(1)} %fusion.88), channel_id=1, source_target_pairs={{0,16},{16,32},{32,48},{48,64},{64,80},{80,96},{96,112},{112,128},... | collective-permute-start | bytes 1544 | tf_op jit(solution)/shard_map/while/body/eval_jaxpr/ppermute | solution.py:14
  241.8 16.0 %collective-permute-start = (bf16[256,2,128]{2,0,1:T(8,128)(2,1)S(1)}, bf16[256,2,128]{2,0,1:T(8,128)(2,1)S(1)}, u32[]{:S(2)}, u32[]{:S(2)}) collective-permute-start(bf16[256,2,128]{2,0,1:T(8,128)(2,1)S(1)} %copy.58), channel_id=1, source_target_pairs={{0,16},{16,32},{32,48},{48,64},{64,80},{80,96},{96,112},{112,128},... | collective-permute-start | bytes 393224 | tf_op jit(solution)/shard_map/while/body/eval_jaxpr/ppermute | solution.py:14
  241.9 15.9 %collective-permute-start.1 = (bf16[256,2,128]{2,0,1:T(8,128)(2,1)S(1)}, bf16[256,2,128]{2,0,1:T(8,128)(2,1)S(1)}, u32[]{:S(2)}, u32[]{:S(2)}) collective-permute-start(bf16[256,2,128]{2,0,1:T(8,128)(2,1)S(1)} %copy.59), channel_id=1, source_target_pairs={{0,16},{16,32},{32,48},{48,64},{64,80},{80,96},{96,112},{112,128},... | collective-permute-start | bytes 393224 | tf_op jit(solution)/shard_map/while/body/eval_jaxpr/ppermute | solution.py:14
  242.0 15.8 %collective-permute-start.2 = (bf16[256]{0:T(256)(128)(2,1)S(1)}, bf16[256]{0:T(256)(128)(2,1)S(1)}, u32[]{:S(2)}, u32[]{:S(2)}) collective-permute-start(bf16[256]{0:T(256)(128)(2,1)S(1)} %copy.60), channel_id=1, source_target_pairs={{0,16},{16,32},{32,48},{48,64},{64,80},{80,96},{96,112},{112,128},... | collective-permute-start | bytes 1544 | tf_op jit(solution)/shard_map/while/body/eval_jaxpr/ppermute | solution.py:14
  242.9 9.2 %collective-permute-start.3 = (bf16[256,2,128]{2,0,1:T(8,128)(2,1)S(1)}, bf16[256,2,128]{2,0,1:T(8,128)(2,1)S(1)}, u32[]{:S(2)}, u32[]{:S(2)}) collective-permute-start(bf16[256,2,128]{2,0,1:T(8,128)(2,1)S(1)} %fusion.86), channel_id=1, source_target_pairs={{0,16},{16,32},{32,48},{48,64},{64,80},{80,96},{96,112},{112,128},... | collective-permute-start | bytes 393224 | tf_op jit(solution)/shard_map/while/body/eval_jaxpr/ppermute | solution.py:14
  257.8 15.7 %collective-permute-start = (bf16[256,2,128]{2,0,1:T(8,128)(2,1)S(1)}, bf16[256,2,128]{2,0,1:T(8,128)(2,1)S(1)}, u32[]{:S(2)}, u32[]{:S(2)}) collective-permute-start(bf16[256,2,128]{2,0,1:T(8,128)(2,1)S(1)} %copy.58), channel_id=1, source_target_pairs={{0,16},{16,32},{32,48},{48,64},{64,80},{80,96},{96,112},{112,128},... | collective-permute-start | bytes 393224 | tf_op jit(solution)/shard_map/while/body/eval_jaxpr/ppermute | solution.py:14
  257.9 15.6 %collective-permute-start.1 = (bf16[256,2,128]{2,0,1:T(8,128)(2,1)S(1)}, bf16[256,2,128]{2,0,1:T(8,128)(2,1)S(1)}, u32[]{:S(2)}, u32[]{:S(2)}) collective-permute-start(bf16[256,2,128]{2,0,1:T(8,128)(2,1)S(1)} %copy.59), channel_id=1, source_target_pairs={{0,16},{16,32},{32,48},{48,64},{64,80},{80,96},{96,112},{112,128},... | collective-permute-start | bytes 393224 | tf_op jit(solution)/shard_map/while/body/eval_jaxpr/ppermute | solution.py:14
  258.0 15.4 %collective-permute-start.2 = (bf16[256]{0:T(256)(128)(2,1)S(1)}, bf16[256]{0:T(256)(128)(2,1)S(1)}, u32[]{:S(2)}, u32[]{:S(2)}) collective-permute-start(bf16[256]{0:T(256)(128)(2,1)S(1)} %copy.60), channel_id=1, source_target_pairs={{0,16},{16,32},{32,48},{48,64},{64,80},{80,96},{96,112},{112,128},... | collective-permute-start | bytes 1544 | tf_op jit(solution)/shard_map/while/body/eval_jaxpr/ppermute | solution.py:14
  273.5 17.9 %collective-permute-start = (bf16[256,2,128]{2,0,1:T(8,128)(2,1)S(1)}, bf16[256,2,128]{2,0,1:T(8,128)(2,1)S(1)}, u32[]{:S(2)}, u32[]{:S(2)}) collective-permute-start(bf16[256,2,128]{2,0,1:T(8,128)(2,1)S(1)} %copy.58), channel_id=1, source_target_pairs={{0,16},{16,32},{32,48},{48,64},{64,80},{80,96},{96,112},{112,128},... | collective-permute-start | bytes 393224 | tf_op jit(solution)/shard_map/while/body/eval_jaxpr/ppermute | solution.py:14
  273.6 17.8 %collective-permute-start.1 = (bf16[256,2,128]{2,0,1:T(8,128)(2,1)S(1)}, bf16[256,2,128]{2,0,1:T(8,128)(2,1)S(1)}, u32[]{:S(2)}, u32[]{:S(2)}) collective-permute-start(bf16[256,2,128]{2,0,1:T(8,128)(2,1)S(1)} %copy.59), channel_id=1, source_target_pairs={{0,16},{16,32},{32,48},{48,64},{64,80},{80,96},{96,112},{112,128},... | collective-permute-start | bytes 393224 | tf_op jit(solution)/shard_map/while/body/eval_jaxpr/ppermute | solution.py:14
  273.7 17.7 %collective-permute-start.2 = (bf16[256]{0:T(256)(128)(2,1)S(1)}, bf16[256]{0:T(256)(128)(2,1)S(1)}, u32[]{:S(2)}, u32[]{:S(2)}) collective-permute-start(bf16[256]{0:T(256)(128)(2,1)S(1)} %copy.60), channel_id=1, source_target_pairs={{0,16},{16,32},{32,48},{48,64},{64,80},{80,96},{96,112},{112,128},... | collective-permute-start | bytes 1544 | tf_op jit(solution)/shard_map/while/body/eval_jaxpr/ppermute | solution.py:14
  274.6 9.4 %collective-permute-start.3 = (bf16[256,2,128]{2,0,1:T(8,128)(2,1)S(1)}, bf16[256,2,128]{2,0,1:T(8,128)(2,1)S(1)}, u32[]{:S(2)}, u32[]{:S(2)}) collective-permute-start(bf16[256,2,128]{2,0,1:T(8,128)(2,1)S(1)} %fusion.86), channel_id=1, source_target_pairs={{0,16},{16,32},{32,48},{48,64},{64,80},{80,96},{96,112},{112,128},... | collective-permute-start | bytes 393224 | tf_op jit(solution)/shard_map/while/body/eval_jaxpr/ppermute | solution.py:14
  291.5 15.8 %collective-permute-start = (bf16[256,2,128]{2,0,1:T(8,128)(2,1)S(1)}, bf16[256,2,128]{2,0,1:T(8,128)(2,1)S(1)}, u32[]{:S(2)}, u32[]{:S(2)}) collective-permute-start(bf16[256,2,128]{2,0,1:T(8,128)(2,1)S(1)} %copy.58), channel_id=1, source_target_pairs={{0,16},{16,32},{32,48},{48,64},{64,80},{80,96},{96,112},{112,128},... | collective-permute-start | bytes 393224 | tf_op jit(solution)/shard_map/while/body/eval_jaxpr/ppermute | solution.py:14
  291.6 15.7 %collective-permute-start.1 = (bf16[256,2,128]{2,0,1:T(8,128)(2,1)S(1)}, bf16[256,2,128]{2,0,1:T(8,128)(2,1)S(1)}, u32[]{:S(2)}, u32[]{:S(2)}) collective-permute-start(bf16[256,2,128]{2,0,1:T(8,128)(2,1)S(1)} %copy.59), channel_id=1, source_target_pairs={{0,16},{16,32},{32,48},{48,64},{64,80},{80,96},{96,112},{112,128},... | collective-permute-start | bytes 393224 | tf_op jit(solution)/shard_map/while/body/eval_jaxpr/ppermute | solution.py:14
  291.7 15.5 %collective-permute-start.2 = (bf16[256]{0:T(256)(128)(2,1)S(1)}, bf16[256]{0:T(256)(128)(2,1)S(1)}, u32[]{:S(2)}, u32[]{:S(2)}) collective-permute-start(bf16[256]{0:T(256)(128)(2,1)S(1)} %copy.60), channel_id=1, source_target_pairs={{0,16},{16,32},{32,48},{48,64},{64,80},{80,96},{96,112},{112,128},... | collective-permute-start | bytes 1544 | tf_op jit(solution)/shard_map/while/body/eval_jaxpr/ppermute | solution.py:14
  307.3 14.8 %collective-permute-start = (bf16[256,2,128]{2,0,1:T(8,128)(2,1)S(1)}, bf16[256,2,128]{2,0,1:T(8,128)(2,1)S(1)}, u32[]{:S(2)}, u32[]{:S(2)}) collective-permute-start(bf16[256,2,128]{2,0,1:T(8,128)(2,1)S(1)} %copy.58), channel_id=1, source_target_pairs={{0,16},{16,32},{32,48},{48,64},{64,80},{80,96},{96,112},{112,128},... | collective-permute-start | bytes 393224 | tf_op jit(solution)/shard_map/while/body/eval_jaxpr/ppermute | solution.py:14
  307.4 14.7 %collective-permute-start.1 = (bf16[256,2,128]{2,0,1:T(8,128)(2,1)S(1)}, bf16[256,2,128]{2,0,1:T(8,128)(2,1)S(1)}, u32[]{:S(2)}, u32[]{:S(2)}) collective-permute-start(bf16[256,2,128]{2,0,1:T(8,128)(2,1)S(1)} %copy.59), channel_id=1, source_target_pairs={{0,16},{16,32},{32,48},{48,64},{64,80},{80,96},{96,112},{112,128},... | collective-permute-start | bytes 393224 | tf_op jit(solution)/shard_map/while/body/eval_jaxpr/ppermute | solution.py:14
  307.5 14.6 %collective-permute-start.2 = (bf16[256]{0:T(256)(128)(2,1)S(1)}, bf16[256]{0:T(256)(128)(2,1)S(1)}, u32[]{:S(2)}, u32[]{:S(2)}) collective-permute-start(bf16[256]{0:T(256)(128)(2,1)S(1)} %copy.60), channel_id=1, source_target_pairs={{0,16},{16,32},{32,48},{48,64},{64,80},{80,96},{96,112},{112,128},... | collective-permute-start | bytes 1544 | tf_op jit(solution)/shard_map/while/body/eval_jaxpr/ppermute | solution.py:14
  322.2 17.5 %collective-permute-start = (bf16[256,2,128]{2,0,1:T(8,128)(2,1)S(1)}, bf16[256,2,128]{2,0,1:T(8,128)(2,1)S(1)}, u32[]{:S(2)}, u32[]{:S(2)}) collective-permute-start(bf16[256,2,128]{2,0,1:T(8,128)(2,1)S(1)} %copy.58), channel_id=1, source_target_pairs={{0,16},{16,32},{32,48},{48,64},{64,80},{80,96},{96,112},{112,128},... | collective-permute-start | bytes 393224 | tf_op jit(solution)/shard_map/while/body/eval_jaxpr/ppermute | solution.py:14
  322.3 17.4 %collective-permute-start.1 = (bf16[256,2,128]{2,0,1:T(8,128)(2,1)S(1)}, bf16[256,2,128]{2,0,1:T(8,128)(2,1)S(1)}, u32[]{:S(2)}, u32[]{:S(2)}) collective-permute-start(bf16[256,2,128]{2,0,1:T(8,128)(2,1)S(1)} %copy.59), channel_id=1, source_target_pairs={{0,16},{16,32},{32,48},{48,64},{64,80},{80,96},{96,112},{112,128},... | collective-permute-start | bytes 393224 | tf_op jit(solution)/shard_map/while/body/eval_jaxpr/ppermute | solution.py:14
  322.4 17.2 %collective-permute-start.2 = (bf16[256]{0:T(256)(128)(2,1)S(1)}, bf16[256]{0:T(256)(128)(2,1)S(1)}, u32[]{:S(2)}, u32[]{:S(2)}) collective-permute-start(bf16[256]{0:T(256)(128)(2,1)S(1)} %copy.60), channel_id=1, source_target_pairs={{0,16},{16,32},{32,48},{48,64},{64,80},{80,96},{96,112},{112,128},... | collective-permute-start | bytes 1544 | tf_op jit(solution)/shard_map/while/body/eval_jaxpr/ppermute | solution.py:14
  323.4 10.2 %collective-permute-start.3 = (bf16[256,2,128]{2,0,1:T(8,128)(2,1)S(1)}, bf16[256,2,128]{2,0,1:T(8,128)(2,1)S(1)}, u32[]{:S(2)}, u32[]{:S(2)}) collective-permute-start(bf16[256,2,128]{2,0,1:T(8,128)(2,1)S(1)} %fusion.86), channel_id=1, source_target_pairs={{0,16},{16,32},{32,48},{48,64},{64,80},{80,96},{96,112},{112,128},... | collective-permute-start | bytes 393224 | tf_op jit(solution)/shard_map/while/body/eval_jaxpr/ppermute | solution.py:14
  339.7 19.7 %collective-permute-start = (bf16[256,2,128]{2,0,1:T(8,128)(2,1)S(1)}, bf16[256,2,128]{2,0,1:T(8,128)(2,1)S(1)}, u32[]{:S(2)}, u32[]{:S(2)}) collective-permute-start(bf16[256,2,128]{2,0,1:T(8,128)(2,1)S(1)} %copy.58), channel_id=1, source_target_pairs={{0,16},{16,32},{32,48},{48,64},{64,80},{80,96},{96,112},{112,128},... | collective-permute-start | bytes 393224 | tf_op jit(solution)/shard_map/while/body/eval_jaxpr/ppermute | solution.py:14
  339.8 19.6 %collective-permute-start.1 = (bf16[256,2,128]{2,0,1:T(8,128)(2,1)S(1)}, bf16[256,2,128]{2,0,1:T(8,128)(2,1)S(1)}, u32[]{:S(2)}, u32[]{:S(2)}) collective-permute-start(bf16[256,2,128]{2,0,1:T(8,128)(2,1)S(1)} %copy.59), channel_id=1, source_target_pairs={{0,16},{16,32},{32,48},{48,64},{64,80},{80,96},{96,112},{112,128},... | collective-permute-start | bytes 393224 | tf_op jit(solution)/shard_map/while/body/eval_jaxpr/ppermute | solution.py:14
  339.9 19.5 %collective-permute-start.2 = (bf16[256]{0:T(256)(128)(2,1)S(1)}, bf16[256]{0:T(256)(128)(2,1)S(1)}, u32[]{:S(2)}, u32[]{:S(2)}) collective-permute-start(bf16[256]{0:T(256)(128)(2,1)S(1)} %copy.60), channel_id=1, source_target_pairs={{0,16},{16,32},{32,48},{48,64},{64,80},{80,96},{96,112},{112,128},... | collective-permute-start | bytes 1544 | tf_op jit(solution)/shard_map/while/body/eval_jaxpr/ppermute | solution.py:14
  340.9 12.3 %collective-permute-start.3 = (bf16[256,2,128]{2,0,1:T(8,128)(2,1)S(1)}, bf16[256,2,128]{2,0,1:T(8,128)(2,1)S(1)}, u32[]{:S(2)}, u32[]{:S(2)}) collective-permute-start(bf16[256,2,128]{2,0,1:T(8,128)(2,1)S(1)} %fusion.86), channel_id=1, source_target_pairs={{0,16},{16,32},{32,48},{48,64},{64,80},{80,96},{96,112},{112,128},... | collective-permute-start | bytes 393224 | tf_op jit(solution)/shard_map/while/body/eval_jaxpr/ppermute | solution.py:14
  343.2 9.6 %collective-permute-start.5 = (bf16[256]{0:T(256)(128)(2,1)S(1)}, bf16[256]{0:T(256)(128)(2,1)S(1)}, u32[]{:S(2)}, u32[]{:S(2)}) collective-permute-start(bf16[256]{0:T(256)(128)(2,1)S(1)} %fusion.88), channel_id=1, source_target_pairs={{0,16},{16,32},{32,48},{48,64},{64,80},{80,96},{96,112},{112,128},... | collective-permute-start | bytes 1544 | tf_op jit(solution)/shard_map/while/body/eval_jaxpr/ppermute | solution.py:14
  359.4 17.2 %collective-permute-start = (bf16[256,2,128]{2,0,1:T(8,128)(2,1)S(1)}, bf16[256,2,128]{2,0,1:T(8,128)(2,1)S(1)}, u32[]{:S(2)}, u32[]{:S(2)}) collective-permute-start(bf16[256,2,128]{2,0,1:T(8,128)(2,1)S(1)} %copy.58), channel_id=1, source_target_pairs={{0,16},{16,32},{32,48},{48,64},{64,80},{80,96},{96,112},{112,128},... | collective-permute-start | bytes 393224 | tf_op jit(solution)/shard_map/while/body/eval_jaxpr/ppermute | solution.py:14
  359.5 17.1 %collective-permute-start.1 = (bf16[256,2,128]{2,0,1:T(8,128)(2,1)S(1)}, bf16[256,2,128]{2,0,1:T(8,128)(2,1)S(1)}, u32[]{:S(2)}, u32[]{:S(2)}) collective-permute-start(bf16[256,2,128]{2,0,1:T(8,128)(2,1)S(1)} %copy.59), channel_id=1, source_target_pairs={{0,16},{16,32},{32,48},{48,64},{64,80},{80,96},{96,112},{112,128},... | collective-permute-start | bytes 393224 | tf_op jit(solution)/shard_map/while/body/eval_jaxpr/ppermute | solution.py:14
  359.6 17.0 %collective-permute-start.2 = (bf16[256]{0:T(256)(128)(2,1)S(1)}, bf16[256]{0:T(256)(128)(2,1)S(1)}, u32[]{:S(2)}, u32[]{:S(2)}) collective-permute-start(bf16[256]{0:T(256)(128)(2,1)S(1)} %copy.60), channel_id=1, source_target_pairs={{0,16},{16,32},{32,48},{48,64},{64,80},{80,96},{96,112},{112,128},... | collective-permute-start | bytes 1544 | tf_op jit(solution)/shard_map/while/body/eval_jaxpr/ppermute | solution.py:14
  360.6 10.4 %collective-permute-start.3 = (bf16[256,2,128]{2,0,1:T(8,128)(2,1)S(1)}, bf16[256,2,128]{2,0,1:T(8,128)(2,1)S(1)}, u32[]{:S(2)}, u32[]{:S(2)}) collective-permute-start(bf16[256,2,128]{2,0,1:T(8,128)(2,1)S(1)} %fusion.86), channel_id=1, source_target_pairs={{0,16},{16,32},{32,48},{48,64},{64,80},{80,96},{96,112},{112,128},... | collective-permute-start | bytes 393224 | tf_op jit(solution)/shard_map/while/body/eval_jaxpr/ppermute | solution.py:14
  360.7 10.0 %collective-permute-start.5 = (bf16[256]{0:T(256)(128)(2,1)S(1)}, bf16[256]{0:T(256)(128)(2,1)S(1)}, u32[]{:S(2)}, u32[]{:S(2)}) collective-permute-start(bf16[256]{0:T(256)(128)(2,1)S(1)} %fusion.88), channel_id=1, source_target_pairs={{0,16},{16,32},{32,48},{48,64},{64,80},{80,96},{96,112},{112,128},... | collective-permute-start | bytes 1544 | tf_op jit(solution)/shard_map/while/body/eval_jaxpr/ppermute | solution.py:14
  376.7 15.1 %collective-permute-start = (bf16[256,2,128]{2,0,1:T(8,128)(2,1)S(1)}, bf16[256,2,128]{2,0,1:T(8,128)(2,1)S(1)}, u32[]{:S(2)}, u32[]{:S(2)}) collective-permute-start(bf16[256,2,128]{2,0,1:T(8,128)(2,1)S(1)} %copy.58), channel_id=1, source_target_pairs={{0,16},{16,32},{32,48},{48,64},{64,80},{80,96},{96,112},{112,128},... | collective-permute-start | bytes 393224 | tf_op jit(solution)/shard_map/while/body/eval_jaxpr/ppermute | solution.py:14
  376.8 15.0 %collective-permute-start.1 = (bf16[256,2,128]{2,0,1:T(8,128)(2,1)S(1)}, bf16[256,2,128]{2,0,1:T(8,128)(2,1)S(1)}, u32[]{:S(2)}, u32[]{:S(2)}) collective-permute-start(bf16[256,2,128]{2,0,1:T(8,128)(2,1)S(1)} %copy.59), channel_id=1, source_target_pairs={{0,16},{16,32},{32,48},{48,64},{64,80},{80,96},{96,112},{112,128},... | collective-permute-start | bytes 393224 | tf_op jit(solution)/shard_map/while/body/eval_jaxpr/ppermute | solution.py:14
  376.9 14.9 %collective-permute-start.2 = (bf16[256]{0:T(256)(128)(2,1)S(1)}, bf16[256]{0:T(256)(128)(2,1)S(1)}, u32[]{:S(2)}, u32[]{:S(2)}) collective-permute-start(bf16[256]{0:T(256)(128)(2,1)S(1)} %copy.60), channel_id=1, source_target_pairs={{0,16},{16,32},{32,48},{48,64},{64,80},{80,96},{96,112},{112,128},... | collective-permute-start | bytes 1544 | tf_op jit(solution)/shard_map/while/body/eval_jaxpr/ppermute | solution.py:14
  391.9 17.0 %collective-permute-start = (bf16[256,2,128]{2,0,1:T(8,128)(2,1)S(1)}, bf16[256,2,128]{2,0,1:T(8,128)(2,1)S(1)}, u32[]{:S(2)}, u32[]{:S(2)}) collective-permute-start(bf16[256,2,128]{2,0,1:T(8,128)(2,1)S(1)} %copy.58), channel_id=1, source_target_pairs={{0,16},{16,32},{32,48},{48,64},{64,80},{80,96},{96,112},{112,128},... | collective-permute-start | bytes 393224 | tf_op jit(solution)/shard_map/while/body/eval_jaxpr/ppermute | solution.py:14
  392.0 16.9 %collective-permute-start.1 = (bf16[256,2,128]{2,0,1:T(8,128)(2,1)S(1)}, bf16[256,2,128]{2,0,1:T(8,128)(2,1)S(1)}, u32[]{:S(2)}, u32[]{:S(2)}) collective-permute-start(bf16[256,2,128]{2,0,1:T(8,128)(2,1)S(1)} %copy.59), channel_id=1, source_target_pairs={{0,16},{16,32},{32,48},{48,64},{64,80},{80,96},{96,112},{112,128},... | collective-permute-start | bytes 393224 | tf_op jit(solution)/shard_map/while/body/eval_jaxpr/ppermute | solution.py:14
  392.1 16.8 %collective-permute-start.2 = (bf16[256]{0:T(256)(128)(2,1)S(1)}, bf16[256]{0:T(256)(128)(2,1)S(1)}, u32[]{:S(2)}, u32[]{:S(2)}) collective-permute-start(bf16[256]{0:T(256)(128)(2,1)S(1)} %copy.60), channel_id=1, source_target_pairs={{0,16},{16,32},{32,48},{48,64},{64,80},{80,96},{96,112},{112,128},... | collective-permute-start | bytes 1544 | tf_op jit(solution)/shard_map/while/body/eval_jaxpr/ppermute | solution.py:14
  409.0 17.9 %collective-permute-start = (bf16[256,2,128]{2,0,1:T(8,128)(2,1)S(1)}, bf16[256,2,128]{2,0,1:T(8,128)(2,1)S(1)}, u32[]{:S(2)}, u32[]{:S(2)}) collective-permute-start(bf16[256,2,128]{2,0,1:T(8,128)(2,1)S(1)} %copy.58), channel_id=1, source_target_pairs={{0,16},{16,32},{32,48},{48,64},{64,80},{80,96},{96,112},{112,128},... | collective-permute-start | bytes 393224 | tf_op jit(solution)/shard_map/while/body/eval_jaxpr/ppermute | solution.py:14
  409.1 17.8 %collective-permute-start.1 = (bf16[256,2,128]{2,0,1:T(8,128)(2,1)S(1)}, bf16[256,2,128]{2,0,1:T(8,128)(2,1)S(1)}, u32[]{:S(2)}, u32[]{:S(2)}) collective-permute-start(bf16[256,2,128]{2,0,1:T(8,128)(2,1)S(1)} %copy.59), channel_id=1, source_target_pairs={{0,16},{16,32},{32,48},{48,64},{64,80},{80,96},{96,112},{112,128},... | collective-permute-start | bytes 393224 | tf_op jit(solution)/shard_map/while/body/eval_jaxpr/ppermute | solution.py:14
  409.2 17.7 %collective-permute-start.2 = (bf16[256]{0:T(256)(128)(2,1)S(1)}, bf16[256]{0:T(256)(128)(2,1)S(1)}, u32[]{:S(2)}, u32[]{:S(2)}) collective-permute-start(bf16[256]{0:T(256)(128)(2,1)S(1)} %copy.60), channel_id=1, source_target_pairs={{0,16},{16,32},{32,48},{48,64},{64,80},{80,96},{96,112},{112,128},... | collective-permute-start | bytes 1544 | tf_op jit(solution)/shard_map/while/body/eval_jaxpr/ppermute | solution.py:14
  410.1 9.4 %collective-permute-start.3 = (bf16[256,2,128]{2,0,1:T(8,128)(2,1)S(1)}, bf16[256,2,128]{2,0,1:T(8,128)(2,1)S(1)}, u32[]{:S(2)}, u32[]{:S(2)}) collective-permute-start(bf16[256,2,128]{2,0,1:T(8,128)(2,1)S(1)} %fusion.86), channel_id=1, source_target_pairs={{0,16},{16,32},{32,48},{48,64},{64,80},{80,96},{96,112},{112,128},... | collective-permute-start | bytes 393224 | tf_op jit(solution)/shard_map/while/body/eval_jaxpr/ppermute | solution.py:14
  (39 other events, 662.5 us)
Sparse Core Ops, SparseCore 0:
  10.4 66.0 all-gather.3
  78.8 68.6 all-gather.5
where the time goes:
time: 556 us; the launch traced here: 555 us
  waiting for transfers between devices  305 us (55%)
  blocking collectives  149 us (27%)
  matrix products  35.8 us (6%)
  starting transfers between devices  33.2 us (6%)
  between operations  14.9 us (3%)
  local copies, waits for them, and re-layouts  11.8 us (2%)
    ppermute x96, waiting for transfers between devices, passed_along(): lax.ppermute(value, axis, [(i, (i + by) % size) for i in range(size)])  211 us
    psum x1, blocking collectives, shards(): grad_table = lax.psum(table_term, ('ctx', 'head', 'req'))  119 us
    all_gather x1, waiting for transfers between devices, shards(): lax.all_gather(value_blk, 'ctx', axis=0, tiled=True)  62.9 us
    ppermute x96, starting transfers between devices, passed_along(): lax.ppermute(value, axis, [(i, (i + by) % size) for i in range(size)])  33.1 us
    all_gather x1, waiting for transfers between devices, shards(): lax.all_gather(key_blk, 'ctx', axis=0, tiled=True)  30.9 us
    all_gather x1, blocking collectives, shards(): lax.all_gather(bias_blk, 'ctx', axis=0, tiled=True)  30.9 us
  transfers between devices with their start and end apart: 98, of which 34 were waited for; matrix products, arithmetic and copies ran while one was open for 6% of the time, Pallas kernels for 0%

commit v1 on v0

v1 whole, which is shorter than its diff:
```python
import functools

import jax
import jax.numpy as jnp
from jax import lax
from jax.experimental import pallas as pl
from jax.experimental.pallas import tpu as pltpu
from jax.sharding import PartitionSpec as P

HD = 128
Z = 8
SCALE = 128.0 ** (-0.5)
LOG2E = 1.4426950408889634
MESH = pl.DeviceIdType.MESH
F32 = jnp.float32
BF16 = jnp.bfloat16
NT = (((1,), (1,)), ((), ()))
TN = (((0,), (0,)), ((), ()))
NN = (((1,), (0,)), ((), ()))


def kernel(
    n_head, n_req, cand, pre, group, kv, levels,
    counts_ref, table_ref, index_ref, q_hbm, k_hbm, v_hbm, o_hbm,
    dq_hbm, dk_hbm, dv_hbm, dt_ref,
    qo, ks, vs, kt, idx_par, bias, onehot,
    probs, dprobs, peaks, st_loc, st_in, st_fin, st_out,
    dq_tmp, rs_out, rs_in, dq_done, dk_acc, dv_acc, col, kv_out, kv_in, kv_done,
    t_loc, t_in1, t_in2, t_in3, t_mid,
    in_sem, out_sem, kv_send, kv_recv, ix_send, ix_recv,
    ag_send, ag_recv, sa_send, sa_recv, sb_send, sb_recv,
    rs_send, rs_recv, dk_send, dk_recv,
    t1_send, t1_recv, t2_send, t2_recv, t3_send, t3_recv,
):
    rows = group * cand
    half = rows // 2
    lanes = rows // HD
    ctx = lax.axis_index("ctx")
    head = lax.axis_index("head")
    req = lax.axis_index("req")
    y = ctx // Z
    z = ctx % Z

    def along_z(by):
        return {"ctx": y * Z + (z + by) % Z}

    partner = {"ctx": (1 - y) * Z + z}
    right, left = along_z(1), along_z(Z - 1)
    t2_codes = [(a, b) for a in range(2) for b in range(n_req) if (a, b) != (0, 0)]

    def t2_peer(a, b):
        return {"ctx": ((y + a) % 2) * Z + z, "req": (req + b) % n_req}

    def t3_peer(b):
        return {"head": (head + b) % n_head}

    loads = []
    for g in range(kv):
        for j in range(group):
            lo = (g * group + j) * HD
            for part, src in ((0, q_hbm), (1, o_hbm)):
                loads.append(pltpu.make_async_copy(
                    src.at[0, :, pl.ds(lo, HD)],
                    qo.at[0, g, part, pl.ds(j * cand, cand), :],
                    in_sem.at[len(loads)]))
        for src, dst in ((k_hbm, ks), (v_hbm, vs)):
            loads.append(pltpu.make_async_copy(
                src.at[0, :, pl.ds(g * HD, HD)],
                dst.at[g, pl.ds(0, pre), :],
                in_sem.at[len(loads)]))
    for copy in loads:
        copy.start()

    barrier = pltpu.get_barrier_semaphore()
    peers = [along_z(o) for o in range(1, Z)]
    peers += [t2_peer(a, b) for a, b in t2_codes]
    peers += [t3_peer(b) for b in range(1, n_head)]
    for peer in peers:
        pl.semaphore_signal(barrier, inc=1, device_id=peer, device_id_type=MESH)

    rs_in[:, :, 0] = jnp.zeros_like(rs_in[:, :, 0])
    dk_acc[...] = jnp.zeros_like(dk_acc)
    dv_acc[...] = jnp.zeros_like(dv_acc)
    col[...] = jnp.zeros_like(col)

    for copy in loads:
        copy.wait()
    live = counts_ref[0] - ctx * cand
    slot = lax.rem(lax.broadcasted_iota(jnp.int32, (rows, HD), 0), cand)
    for g in range(kv):
        qo[0, g, 1] = jnp.where(slot < live, qo[0, g, 1], jnp.zeros((rows, HD), BF16))

    pl.semaphore_wait(barrier, len(peers))

    def remote(src, dst, send, recv, device):
        return pltpu.make_async_remote_copy(
            src_ref=src, dst_ref=dst, send_sem=send, recv_sem=recv,
            device_id=device, device_id_type=MESH)

    def gather(g, way, step, part):
        if way == 0:
            src, dst, device = lax.rem(9 - step, Z), Z - step, right
        else:
            src, dst, device = step - 1, step, left
        return remote(
            qo.at[src, g, part], qo.at[dst, g, part],
            ag_send.at[g, way, part, step - 1], ag_recv.at[g, way, part, step - 1], device)

    def kv_copy(g, which):
        ref = (ks, vs)[which]
        return remote(
            ref.at[g, pl.ds(0, pre), :], ref.at[g, pl.ds(pre, pre), :],
            kv_send.at[g, which], kv_recv.at[g, which], partner)

    ix_copy = remote(index_ref, idx_par, ix_send, ix_recv, partner)

    def stat_a(g, o):
        return remote(
            st_loc.at[g, o], st_in.at[g, o],
            sa_send.at[g, o], sa_recv.at[g, o], along_z(o))

    def stat_b(g, o):
        return remote(
            st_out.at[g], st_fin.at[g, Z - o],
            sb_send.at[g, o], sb_recv.at[g, o], along_z(o))

    def scatter_half(g, way):
        at = pl.ds(way * half, half)
        return remote(
            rs_out.at[g, way, 0, at, :], rs_in.at[g, way, 0, at, :],
            rs_send.at[g, way, 0], rs_recv.at[g, way, 0], (left, right)[way])

    def scatter(g, way, step):
        return remote(
            rs_out.at[g, way, step], rs_in.at[g, way, step],
            rs_send.at[g, way, step], rs_recv.at[g, way, step], (left, right)[way])

    def kv_grad(g, which):
        return remote(
            kv_out.at[g, which], kv_in.at[g, which],
            dk_send.at[g, which], dk_recv.at[g, which], partner)

    def t1_copy(o):
        return remote(t_loc, t_in1.at[o], t1_send.at[o], t1_recv.at[o], along_z(o))

    def t2_copy(i):
        return remote(
            t_mid.at[0], t_in2.at[i], t2_send.at[i], t2_recv.at[i], t2_peer(*t2_codes[i]))

    def t3_copy(b):
        return remote(t_mid.at[1], t_in3.at[b], t3_send.at[b], t3_recv.at[b], t3_peer(b))

    ix_copy.start()
    for g in range(kv):
        for which in range(2):
            kv_copy(g, which).start()
    for part in range(2):
        for way in range(2):
            gather(0, way, 1, part).start()

    level = lax.broadcasted_iota(jnp.int32, (levels, HD), 0)
    table = jnp.zeros((levels, HD), F32)
    for i in range(levels):
        table = jnp.where(level == i, table_ref[i], table)
    table = table.astype(BF16)

    def offsets(index, place):
        hot = (lax.broadcasted_iota(jnp.int32, (levels, pre), 0) == index).astype(F32)
        onehot[place] = hot
        bias[pl.ds(place * pre, pre), :] = lax.dot_general(
            hot.astype(BF16), table, TN, preferred_element_type=F32) * LOG2E

    offsets(index_ref[...], 0)
    ix_copy.wait()
    offsets(idx_par[...], 1)

    def split(row):
        return [row[:, i * HD:(i + 1) * HD] for i in range(lanes)]

    def first_pass(g, s):
        q_blk = qo[s, g, 0]
        o_blk = qo[s, g, 1]
        off = jnp.concatenate([bias[...]] * lanes, axis=1)
        scores = lax.dot_general(ks[g], q_blk, NT, preferred_element_type=F32)
        scores = scores * (SCALE * LOG2E) + off
        peak = jnp.max(scores, axis=0, keepdims=True)
        prob = jnp.exp2(scores - peak)
        total = jnp.sum(prob, axis=0, keepdims=True)
        dprob = lax.dot_general(vs[g], o_blk, NT, preferred_element_type=F32)
        delta = jnp.sum(prob * dprob, axis=0, keepdims=True) / total
        probs[g, s] = prob
        dprobs[g, s] = dprob
        peaks[g, s] = peak
        lse = peak + jnp.log2(total)
        st_loc[g, s] = jnp.concatenate(split(lse) + split(delta), axis=0)

    def combine(g):
        st_in[g, 0] = st_loc[g, 0]
        parts = st_in[g]
        lse = parts[:, 0:lanes]
        top = jnp.max(lse, axis=0, keepdims=True)
        total = top + jnp.log2(jnp.sum(jnp.exp2(lse - top), axis=0, keepdims=True))
        weight = jnp.exp2(lse - total)
        delta = jnp.sum(weight * parts[:, lanes:], axis=0)
        both = jnp.concatenate([total[0], delta], axis=0)
        st_out[g] = both
        st_fin[g, 0] = both

    def second_pass(g, s, c):
        fin = st_fin[g, s]
        lse = jnp.concatenate([fin[i:i + 1] for i in range(lanes)], axis=1)
        delta = jnp.concatenate([fin[lanes + i:lanes + i + 1] for i in range(lanes)], axis=1)
        prob = probs[g, s] * jnp.exp2(peaks[g, s] - lse)
        dscore = prob * (dprobs[g, s] - delta)
        col[...] += functools.reduce(lambda a, b: a + b, split(dscore))
        prob_b = prob.astype(BF16)
        dscore_b = dscore.astype(BF16)
        dv_acc[g] += lax.dot_general(prob_b, qo[s, g, 1], NN, preferred_element_type=F32)
        dk_acc[g] += lax.dot_general(dscore_b, qo[s, g, 0], NN, preferred_element_type=F32)
        dq = lax.dot_general(kt[g], dscore_b, NN, preferred_element_type=F32)
        dq_tmp[c] = dq.T

    def kv_finish(g):
        for which, acc, hbm in ((0, dk_acc, dk_hbm), (1, dv_acc, dv_hbm)):
            kv_grad(g, which).wait_recv()
            total = acc[g, 0:pre] + kv_in[g, which].astype(F32)
            if which == 0:
                total = total * SCALE
            kv_done[g, which] = total.astype(BF16)

    def kv_store(g, which):
        hbm = (dk_hbm, dv_hbm)[which]
        return pltpu.make_async_copy(
            kv_done.at[g, which], hbm.at[0, :, pl.ds(g * HD, HD)], out_sem.at[g, which])

    def dq_store(g, j):
        return pltpu.make_async_copy(
            dq_done.at[g, pl.ds(j * cand, cand), :],
            dq_hbm.at[0, :, pl.ds((g * group + j) * HD, HD)],
            out_sem.at[g, 2 + j])

    def tick(t, _):
        phase, k = t // 6, t % 6

        for g in range(kv):
            @pl.when((phase == g) & (k == 0))
            def _():
                if g > 0:
                    for part in range(2):
                        for way in range(2):
                            gather(g, way, 1, part).start()
                for which in range(2):
                    kv_copy(g, which).wait()
                kt[g] = ks[g].astype(F32).T.astype(BF16)

        @pl.when((phase < kv) & (k >= 1) & (k < 4))
        def _():
            for part in range(2):
                for way in range(2):
                    gather(phase, way, k, part).wait_recv()

                    @pl.when((k < 3) | (part == way))
                    def _():
                        gather(phase, way, k + 1, part).start()

        @pl.when((phase < kv) & (k == 4))
        def _():
            gather(phase, 0, 4, 0).wait_recv()
            gather(phase, 1, 4, 1).wait_recv()

        @pl.when((phase < kv) & (k < 5))
        def _():
            def chunk(c, _):
                s = jnp.where(c == 0, (Z - k) % Z, k)
                first_pass(phase, s)
                return 0

            lax.fori_loop(0, jnp.where((k == 0) | (k == 4), 1, 2), chunk, 0)

            @pl.when(k == 4)
            def _():
                for o in range(1, Z):
                    stat_a(phase, o).start()

        h = phase - 1

        @pl.when((phase > 0) & (k == 0))
        def _():
            for o in range(1, Z):
                stat_a(h, o).wait()
            combine(h)
            for o in range(1, Z):
                stat_b(h, o).start()

        @pl.when((phase > 0) & (k > 0))
        def _():
            j = k - 1

            @pl.when(j == 0)
            def _():
                for o in range(1, Z):
                    stat_b(h, o).wait()

            def chunk(c, _):
                s = jnp.where(c == 0, (4 + j) % Z, 4 - j)
                second_pass(h, s, c)

                @pl.when(j == 0)
                def _():
                    for way in range(2):
                        at = pl.ds(way * half, half)
                        rs_out[h, way, 0, at, :] = dq_tmp[0, at, :].astype(BF16)
                        scatter_half(h, way).start()

                for way in range(2):
                    @pl.when((j > 0) & (j < 4) & (c == way))
                    def _():
                        @pl.when(j == 1)
                        def _():
                            scatter_half(h, way).wait_recv()

                        @pl.when(j > 1)
                        def _():
                            scatter(h, way, j - 1).wait_recv()

                        rs_out[h, way, j] = (
                            dq_tmp[way] + rs_in[h, way, j - 1].astype(F32)).astype(BF16)
                        scatter(h, way, j).start()
                return 0

            lax.fori_loop(0, jnp.where((j == 0) | (j == 4), 1, 2), chunk, 0)

            @pl.when(j == 4)
            def _():
                for which, acc in ((0, dk_acc), (1, dv_acc)):
                    kv_out[h, which] = acc[h, pre:2 * pre].astype(BF16)
                    kv_grad(h, which).start()

                @pl.when(phase == kv)
                def _():
                    t_loc[...] = sum(
                        lax.dot_general(
                            onehot[i], col[i * pre:(i + 1) * pre], NN,
                            precision=lax.Precision.HIGHEST, preferred_element_type=F32)
                        for i in range(2))
                    for o in range(1, Z):
                        t1_copy(o).start()

                for way in range(2):
                    scatter(h, way, 3).wait_recv()
                dq = dq_tmp[0] + rs_in[h, 0, 3].astype(F32) + rs_in[h, 1, 3].astype(F32)
                dq_done[h] = (dq * SCALE).astype(BF16)

        for g in range(kv):
            @pl.when((phase == g + 1) & (k == 5))
            def _():
                for j in range(group):
                    dq_store(g, j).start()
        return 0

    lax.fori_loop(0, 6 * (kv + 1), tick, 0)

    for o in range(1, Z):
        t1_copy(o).wait()
    t_mid[0] = t_loc[...] + sum(t_in1[o] for o in range(1, Z))
    for i in range(len(t2_codes)):
        t2_copy(i).start()
    for g in range(kv):
        kv_finish(g)
        for which in range(2):
            kv_store(g, which).start()
    for i in range(len(t2_codes)):
        t2_copy(i).wait()
    total = t_mid[0] + sum(t_in2[i] for i in range(len(t2_codes)))
    if n_head > 1:
        t_mid[1] = total
        for b in range(1, n_head):
            t3_copy(b).start()

    for g in range(kv):
        for way in range(2):
            for part in range(2):
                for step in range(1, 5):
                    if step < 4 or part == way:
                        gather(g, way, step, part).wait_send()
            scatter_half(g, way).wait_send()
            for step in range(1, 4):
                scatter(g, way, step).wait_send()
        for which in range(2):
            kv_grad(g, which).wait_send()
            kv_store(g, which).wait()
        for j in range(group):
            dq_store(g, j).wait()

    if n_head > 1:
        for b in range(1, n_head):
            t3_copy(b).wait()
        total = total + sum(t_in3[b] for b in range(1, n_head))
    total = jnp.sum(total, axis=1, keepdims=True)
    place = lax.broadcasted_iota(jnp.int32, (levels, levels), 0)
    across = lax.broadcasted_iota(jnp.int32, (levels, levels), 1)
    dt_ref[...] = jnp.sum(
        jnp.where(place == across, total, 0.0), axis=0, keepdims=True)


def shards(queries, keys, values, grad_out, counts, rate_table, rate_index):
    n_head, n_req = lax.axis_size("head"), lax.axis_size("req")
    cand, pre = queries.shape[1], keys.shape[1]
    kv = keys.shape[2] // HD
    group = queries.shape[2] // keys.shape[2]
    levels = rate_table.shape[0]
    rows = group * cand
    lanes = rows // HD
    any_ = pl.BlockSpec(memory_space=pl.ANY)
    smem = pl.BlockSpec(memory_space=pltpu.SMEM)
    vmem = pl.BlockSpec(memory_space=pltpu.VMEM)
    dma = pltpu.SemaphoreType.DMA
    out = pl.pallas_call(
        functools.partial(kernel, n_head, n_req, cand, pre, group, kv, levels),
        out_shape=(
            jax.ShapeDtypeStruct(queries.shape, BF16),
            jax.ShapeDtypeStruct(keys.shape, BF16),
            jax.ShapeDtypeStruct(values.shape, BF16),
            jax.ShapeDtypeStruct((1, levels), F32),
        ),
        in_specs=[smem, smem, vmem, any_, any_, any_, any_],
        out_specs=(any_, any_, any_, vmem),
        scratch_shapes=[
            pltpu.VMEM((Z, kv, 2, rows, HD), BF16),
            pltpu.VMEM((kv, 2 * pre, HD), BF16),
            pltpu.VMEM((kv, 2 * pre, HD), BF16),
            pltpu.VMEM((kv, HD, 2 * pre), BF16),
            pltpu.VMEM((1, pre), jnp.int32),
            pltpu.VMEM((2 * pre, HD), F32),
            pltpu.VMEM((2, levels, pre), F32),
            pltpu.VMEM((kv, Z, 2 * pre, rows), F32),
            pltpu.VMEM((kv, Z, 2 * pre, rows), F32),
            pltpu.VMEM((kv, Z, 1, rows), F32),
            pltpu.VMEM((kv, Z, 2 * lanes, HD), F32),
            pltpu.VMEM((kv, Z, 2 * lanes, HD), F32),
            pltpu.VMEM((kv, Z, 2 * lanes, HD), F32),
            pltpu.VMEM((kv, 2 * lanes, HD), F32),
            pltpu.VMEM((2, rows, HD), F32),
            pltpu.VMEM((kv, 2, 4, rows, HD), BF16),
            pltpu.VMEM((kv, 2, 4, rows, HD), BF16),
            pltpu.VMEM((kv, rows, HD), BF16),
            pltpu.VMEM((kv, 2 * pre, HD), F32),
            pltpu.VMEM((kv, 2 * pre, HD), F32),
            pltpu.VMEM((2 * pre, HD), F32),
            pltpu.VMEM((kv, 2, pre, HD), BF16),
            pltpu.VMEM((kv, 2, pre, HD), BF16),
            pltpu.VMEM((kv, 2, pre, HD), BF16),
            pltpu.VMEM((levels, HD), F32),
            pltpu.VMEM((Z, levels, HD), F32),
            pltpu.VMEM((2 * n_req - 1, levels, HD), F32),
            pltpu.VMEM((n_head, levels, HD), F32),
            pltpu.VMEM((2, levels, HD), F32),
            dma((kv * (2 * group + 2),)),
            dma((kv, 2 + group)),
            dma((kv, 2)),
            dma((kv, 2)),
            dma,
            dma,
            dma((kv, 2, 2, 4)),
            dma((kv, 2, 2, 4)),
            dma((kv, Z)),
            dma((kv, Z)),
            dma((kv, Z)),
            dma((kv, Z)),
            dma((kv, 2, 4)),
            dma((kv, 2, 4)),
            dma((kv, 2)),
            dma((kv, 2)),
            dma((Z,)),
            dma((Z,)),
            dma((2 * n_req - 1,)),
            dma((2 * n_req - 1,)),
            dma((n_head,)),
            dma((n_head,)),
        ],
        compiler_params=pltpu.CompilerParams(
            collective_id=0, has_side_effects=True, vmem_limit_bytes=48 * 1024 * 1024),
    )(counts, rate_table, rate_index, queries, keys, values, grad_out)
    return out[0], out[1], out[2], out[3].reshape(levels)


def solution(mesh):
    split = P("req", "ctx", "head")
    return jax.shard_map(
        shards,
        mesh=mesh,
        in_specs=(split, split, split, split, P("req"), P(), P("req", "ctx")),
        out_specs=(split, split, split, P()),
        check_vma=False,
    )
```

time: 556 us -> 94.5 us (0.17)
  waiting for transfers between devices: 305 us -> 0 us
  blocking collectives: 149 us -> 0 us
  Pallas kernels: 0 us -> 86.9 us
  matrix products: 35.8 us -> 0 us
  starting transfers between devices: 33.2 us -> 0 us
  between operations: 14.9 us -> 1.35 us
  local copies, waits for them, and re-layouts: 11.8 us -> 6.1 us
    ppermute x96 -> x0, waiting for transfers between devices: 211 us -> none  [passed_along(): lax.ppermute(value, axis, [(i, (i + by) % size) for i in range(size)])]
    psum x1 -> x0, blocking collectives: 119 us -> none  [shards(): grad_table = lax.psum(table_term, ('ctx', 'head', 'req'))]
    all_gather x2 -> x0, waiting for transfers between devices: 93.8 us -> none  [the longest x1 62.9 us: shards(): lax.all_gather(value_blk, 'ctx', axis=0, tiled=True)]
    pallas_call x0 -> x1, Pallas kernels: none -> 86.9 us  [shards(): pl.pallas_call(functools.partial(kernel, n_head, n_req, cand, pre, group,...]
    dot_general x84 -> x0, matrix products: 35.8 us -> none  [the longest x1 9.12 us: stats_fold(): jnp.einsum('gjcp,pgd->gjcd', weights, value_blk.astype(jnp.float32), prec...]
    ppermute x96 -> x0, starting transfers between devices: 33.1 us -> none  [passed_along(): lax.ppermute(value, axis, [(i, (i + by) % size) for i in range(size)])]
    all_gather x1 -> x0, blocking collectives: 30.9 us -> none  [shards(): lax.all_gather(bias_blk, 'ctx', axis=0, tiled=True)]
  transfers between devices with their start and end apart: 98 -> 0, of which waited for: 34 -> 0; matrix products, arithmetic and copies ran while one was open for 6% -> 0% of each run, Pallas kernels for 0% -> 0%
where the time goes in v1:
time: 94.5 us; the launch traced here: 94.3 us
  Pallas kernels  86.9 us (92%)
  local copies, waits for them, and re-layouts  6.1 us (6%)
  between operations  1.35 us (1%)
    pallas_call x1, Pallas kernels, shards(): pl.pallas_call(functools.partial(kernel, n_head, n_req, cand, pre, group,...  86.9 us
    unnamed x16, local copies, waits for them, and re-layouts  6.1 us

profile of v1, /device:TPU:1, one launch (start us, length us, event | category | flops | bytes accessed | tf_op | source)
XLA Modules:
  0.0 94.3 jit_solution(61757723871897688)
XLA Ops:
  0.6 0.0 copy-start.4
  0.6 0.0 copy-start.5
  1.3 0.0 copy-done.4
  1.3 0.0 copy-done.5
  1.3 0.0 copy-start
  1.3 0.9 copy-done
  2.2 0.0 copy-start.1
  2.2 0.9 copy-done.1
  3.1 0.0 copy-start.2
  3.1 0.9 copy-done.2
  4.1 0.0 copy-start.3
  4.1 0.9 copy-done.3
  5.0 86.9 %shard_map.102 = (bf16[1,64,1024]{2,1,0:T(8,128)(2,1)S(1)}, bf16[1,256,256]{2,1,0:T(8,128)(2,1)S(1)}, bf16[1,256,256]{2,1,0:T(8,128)(2,1)S(1)}, f32[1,16]{1,0:T(1,128)S(1)}) custom-call(s32[1]{0:T(128)S(6)} %copy.15.counts_ref, f32[16]{0:T(128)S(1)} %copy-done.5, s32[1,256]{1,0:T(1,128)S(1)} %copy-done.4, bf16[1,64,1024]{2,1,0:T(8,128)(2,1)S(1)} %copy-done, ...), custom_call_target="tpu_custom_call" | custom-call | tf_op jit(solution)/shard_map/pallas_call | solution.py:418
  91.8 0.7 copy.16
  92.5 0.7 copy.17
  93.2 0.7 copy.18
  93.8 0.5 copy.19
Async XLA Ops:
  0.6 0.7 copy-start.4
  0.6 0.7 copy-start.5
  1.3 0.9 copy-start
  2.2 0.9 copy-start.1
  3.1 0.9 copy-start.2
  4.1 0.9 copy-start.3

commit v2 on v1

v2 whole, which is shorter than its diff:
```python
import functools

import jax
import jax.numpy as jnp
from jax import lax
from jax.experimental import pallas as pl
from jax.experimental.pallas import tpu as pltpu
from jax.sharding import PartitionSpec as P

HD = 128
Z = 8
SCALE = 128.0 ** (-0.5)
LOG2E = 1.4426950408889634
MESH = pl.DeviceIdType.MESH
F32 = jnp.float32
BF16 = jnp.bfloat16
NT = (((1,), (1,)), ((), ()))
TN = (((0,), (0,)), ((), ()))
NN = (((1,), (0,)), ((), ()))


def kernel(
    n_head, n_req, cand, pre, group, kv, levels,
    counts_ref, table_ref, index_ref, q_hbm, k_hbm, v_hbm, o_hbm,
    dq_hbm, dk_hbm, dv_hbm, dt_ref,
    qo, ks, vs, kt, idx_par, bias, onehot,
    probs, dprobs, peaks, deltas, fin, lev_a, lev_b, st_loc, st_in, st_all,
    dq_all, rs_out, rs_in, dq_done, dk_acc, dv_acc, kv_out, kv_in, kv_done,
    t_mid, t_in1, t_in2,
    in_sem, out_sem, kv_send, kv_recv, ix_send, ix_recv,
    ag_send, ag_recv, sa_send, sa_recv, sb_send, sb_recv,
    rs_send, rs_recv, dk_send, dk_recv,
    t1_send, t1_recv, t2_send, t2_recv,
):
    rows = group * cand
    half = rows // 2
    lanes = rows // HD
    n_core = min(n_req, 2)
    n_hi = n_req // n_core
    ctx = lax.axis_index("ctx")
    head = lax.axis_index("head")
    req = lax.axis_index("req")
    y = ctx // Z
    z = ctx % Z
    hi = req // n_core
    core = req % n_core

    def along_z(by):
        return {"ctx": y * Z + (z + by) % Z}

    partner = {"ctx": (1 - y) * Z + z}
    right, left = along_z(1), along_z(Z - 1)
    t1_codes = [(a, b) for a in range(Z) for b in range(n_core)][1:]
    t2_codes = [
        (a, b, c) for a in range(n_head) for b in range(2) for c in range(n_hi)][1:]

    def t1_peer(a, b):
        return {"ctx": y * Z + (z + a) % Z, "req": hi * n_core + (core + b) % n_core}

    def t2_peer(a, b, c):
        return {
            "head": (head + a) % n_head,
            "ctx": ((y + b) % 2) * Z + z,
            "req": ((hi + c) % n_hi) * n_core + core,
        }

    barrier = pltpu.get_barrier_semaphore()
    peers = [t1_peer(*code) for code in t1_codes] + [t2_peer(*code) for code in t2_codes]
    for peer in peers:
        pl.semaphore_signal(barrier, inc=1, device_id=peer, device_id_type=MESH)

    loads, late_loads = [], []
    for g in range(kv):
        for j in range(group):
            lo = (g * group + j) * HD
            for part, src in ((0, q_hbm), (1, o_hbm)):
                loads.append(pltpu.make_async_copy(
                    src.at[0, :, pl.ds(lo, HD)],
                    qo.at[0, g, part, pl.ds(j * cand, cand), :],
                    in_sem.at[len(loads)]))
    for g in range(kv):
        for src, dst in ((k_hbm, ks), (v_hbm, vs)):
            late_loads.append(pltpu.make_async_copy(
                src.at[0, :, pl.ds(g * HD, HD)],
                dst.at[g, pl.ds(0, pre), :],
                in_sem.at[len(loads) + len(late_loads)]))
    for copy in loads + late_loads:
        copy.start()

    rs_in[:, :, 0] = jnp.zeros_like(rs_in[:, :, 0])
    dk_acc[...] = jnp.zeros_like(dk_acc)
    dv_acc[...] = jnp.zeros_like(dv_acc)

    level = lax.broadcasted_iota(jnp.int32, (levels, HD), 0)
    table = jnp.zeros((levels, HD), F32)
    for i in range(levels):
        table = jnp.where(level == i, table_ref[i], table)
    table = table.astype(BF16)

    def offsets(index, place):
        hot = (lax.broadcasted_iota(jnp.int32, (levels, pre), 0) == index)
        hot = hot.astype(F32).astype(BF16)
        onehot[:, pl.ds(place * pre, pre)] = hot
        bias[pl.ds(place * pre, pre), :] = lax.dot_general(
            hot, table, TN, preferred_element_type=F32) * LOG2E

    offsets(index_ref[...], 0)

    for copy in loads + late_loads:
        copy.wait()
    live = counts_ref[0] - ctx * cand
    slot = lax.rem(lax.broadcasted_iota(jnp.int32, (rows, HD), 0), cand)
    for g in range(kv):
        qo[0, g, 1] = jnp.where(slot < live, qo[0, g, 1], jnp.zeros((rows, HD), BF16))

    pl.semaphore_wait(barrier, len(peers))

    def remote(src, dst, send, recv, device):
        return pltpu.make_async_remote_copy(
            src_ref=src, dst_ref=dst, send_sem=send, recv_sem=recv,
            device_id=device, device_id_type=MESH)

    def gather(g, way, step, part):
        if way == 0:
            src, dst, device = lax.rem(9 - step, Z), Z - step, right
        else:
            src, dst, device = step - 1, step, left
        return remote(
            qo.at[src, g, part], qo.at[dst, g, part],
            ag_send.at[g, way, part, step - 1], ag_recv.at[g, way, part, step - 1], device)

    def kv_copy(g, which):
        ref = (ks, vs)[which]
        return remote(
            ref.at[g, pl.ds(0, pre), :], ref.at[g, pl.ds(pre, pre), :],
            kv_send.at[g, which], kv_recv.at[g, which], partner)

    ix_copy = remote(index_ref, idx_par, ix_send, ix_recv, partner)

    def stat_a(g, o):
        return remote(
            st_loc.at[g, o], st_in.at[g, o],
            sa_send.at[g, o], sa_recv.at[g, o], along_z(o))

    def stat_b(g, o):
        return remote(
            st_all.at[g, 0], st_all.at[g, o],
            sb_send.at[g, o], sb_recv.at[g, o], along_z(o))

    def scatter(g, way, step, part):
        at = pl.ds(part * half, half)
        return remote(
            rs_out.at[g, way, step, at, :], rs_in.at[g, way, step, at, :],
            rs_send.at[g, way, step, part], rs_recv.at[g, way, step, part],
            (left, right)[way])

    def kv_grad(g, which):
        return remote(
            kv_out.at[g, which], kv_in.at[g, which],
            dk_send.at[g, which], dk_recv.at[g, which], partner)

    def t1_copy(i):
        return remote(
            t_mid.at[0], t_in1.at[i], t1_send.at[i], t1_recv.at[i], t1_peer(*t1_codes[i]))

    def t2_copy(i):
        return remote(
            t_mid.at[1], t_in2.at[i], t2_send.at[i], t2_recv.at[i], t2_peer(*t2_codes[i]))

    for g in range(kv):
        for part in range(2):
            for way in range(2):
                gather(g, way, 1, part).start()
        if g == 0:
            ix_copy.start()
        for which in range(2):
            kv_copy(g, which).start()

    ix_copy.wait()
    offsets(idx_par[...], 1)

    def split(row):
        return [row[:, i * HD:(i + 1) * HD] for i in range(lanes)]

    def joined(block):
        return jnp.concatenate([block[i:i + 1] for i in range(lanes)], axis=1)

    def first_pass(g, s):
        q_blk = qo[s, g, 0]
        o_blk = qo[s, g, 1]
        off = jnp.concatenate([bias[...]] * lanes, axis=1)
        scores = lax.dot_general(ks[g], q_blk, NT, preferred_element_type=F32)
        scores = scores * (SCALE * LOG2E) + off
        peak = jnp.max(scores, axis=0, keepdims=True)
        prob = jnp.exp2(scores - peak)
        total = jnp.sum(prob, axis=0, keepdims=True)
        dprob = lax.dot_general(vs[g], o_blk, NT, preferred_element_type=F32)
        delta = jnp.sum(prob * dprob, axis=0, keepdims=True) / total
        probs[g, s] = prob
        dprobs[g, s] = dprob
        peaks[g, s] = peak
        deltas[g, s] = delta
        lev_a[g, s] = lax.dot_general(
            onehot[...], (prob * (dprob - delta)).astype(BF16), NN,
            preferred_element_type=F32)
        lev_b[g, s] = lax.dot_general(
            onehot[...], prob.astype(BF16), NN, preferred_element_type=F32)
        lse = peak + jnp.log2(total)
        st_loc[g, s] = jnp.concatenate(split(lse) + split(delta), axis=0)

    def merged(parts):
        lse = [p[0:lanes] for p in parts]
        top = functools.reduce(jnp.maximum, lse)
        total = top + jnp.log2(sum(jnp.exp2(v - top) for v in lse))
        delta = sum(jnp.exp2(v - total) * p[lanes:] for v, p in zip(lse, parts))
        return total, delta

    def combine(g):
        total, delta = merged([st_loc[g, 0]] + [st_in[g, o] for o in range(1, Z) if o != 4])
        st_all[g, 0, 0] = jnp.concatenate([total, delta], axis=0)

    def finish(g):
        def one(s, acc):
            total, delta = merged([
                st_all[g, lax.rem(Z - s, Z), 0], st_all[g, lax.rem(12 - s, Z), 1]])
            delta = joined(delta)
            factor = jnp.exp2(peaks[g, s] - joined(total))
            fin[g, s] = jnp.concatenate([factor, delta], axis=0)
            term = factor * (lev_a[g, s] - (delta - deltas[g, s]) * lev_b[g, s])
            return acc + functools.reduce(lambda a, b: a + b, split(term))

        return lax.fori_loop(0, Z, one, jnp.zeros((levels, HD), F32))

    def second_pass(g, s):
        both = fin[g, s]
        prob = probs[g, s] * both[0:1]
        dscore = prob * (dprobs[g, s] - both[1:2])
        prob_b = prob.astype(BF16)
        dscore_b = dscore.astype(BF16)
        dq = lax.dot_general(kt[g], dscore_b, NN, preferred_element_type=F32)
        dq_all[g, s] = dq.T
        dv_acc[g] += lax.dot_general(prob_b, qo[s, g, 1], NN, preferred_element_type=F32)
        dk_acc[g] += lax.dot_general(dscore_b, qo[s, g, 0], NN, preferred_element_type=F32)

    def kv_finish(g):
        for which, acc in ((0, dk_acc), (1, dv_acc)):
            kv_grad(g, which).wait_recv()
            total = acc[g, 0:pre] + kv_in[g, which].astype(F32)
            if which == 0:
                total = total * SCALE
            kv_done[g, which] = total.astype(BF16)
            kv_store(g, which).start()

    def kv_store(g, which):
        hbm = (dk_hbm, dv_hbm)[which]
        return pltpu.make_async_copy(
            kv_done.at[g, which], hbm.at[0, :, pl.ds(g * HD, HD)], out_sem.at[g, which])

    def dq_store(g, j):
        return pltpu.make_async_copy(
            dq_done.at[g, pl.ds(j * cand, cand), :],
            dq_hbm.at[0, :, pl.ds((g * group + j) * HD, HD)],
            out_sem.at[g, 2 + j])

    def gather_tick(t, _):
        k, g = t // kv, t % kv

        for i in range(kv):
            @pl.when((k == 0) & (g == i))
            def _():
                for which in range(2):
                    kv_copy(i, which).wait()
                kt[i] = ks[i].astype(F32).T.astype(BF16)

        @pl.when((k >= 1) & (k < 4))
        def _():
            for part in range(2):
                for way in range(2):
                    gather(g, way, k, part).wait_recv()

                    @pl.when((k < 3) | (part == way))
                    def _():
                        gather(g, way, k + 1, part).start()

        @pl.when(k == 4)
        def _():
            gather(g, 0, 4, 0).wait_recv()
            gather(g, 1, 4, 1).wait_recv()

        def chunk(c, _):
            first_pass(g, jnp.where(c == 0, (Z - k) % Z, k))
            return 0

        lax.fori_loop(0, jnp.where((k == 0) | (k == 4), 1, 2), chunk, 0)

        @pl.when(k == 3)
        def _():
            for o in (5, 3, 6, 2, 7, 1):
                stat_a(g, o).start()

        @pl.when(k == 4)
        def _():
            for o in (5, 3, 6, 2, 7, 1):
                stat_a(g, o).wait()
            combine(g)
            st_all[g, 0, 1] = st_loc[g, 4]
            for o in (4, 5, 3, 6, 2, 7, 1):
                stat_b(g, o).start()

        return 0

    lax.fori_loop(0, 5 * kv, gather_tick, 0)

    def stats(g):
        for o in (1, 7, 2, 6, 3, 5, 4):
            stat_b(g, o).wait()
        term = finish(g)
        t_mid[0] = term if g == 0 else t_mid[0] + term
        if g == kv - 1:
            for i in range(len(t1_codes)):
                t1_copy(i).start()

    def scatter_first(g):
        for way in range(2):
            at = pl.ds(way * half, half)
            rs_out[g, way, 0, at, :] = dq_all[g, 4, at, :].astype(BF16)
            scatter(g, way, 0, way).start()

    def scatter_next(g, step):
        for part in range(2):
            for way in range(2):
                at = pl.ds(part * half, half)
                if step > 1 or part == way:
                    scatter(g, way, step - 1, part).wait_recv()
                s = 4 + step if way == 0 else 4 - step
                rs_out[g, way, step, at, :] = (
                    dq_all[g, s, at, :] + rs_in[g, way, step - 1, at, :].astype(F32)
                ).astype(BF16)
                scatter(g, way, step, part).start()

    def scatter_last(g):
        for part in range(2):
            at = pl.ds(part * half, half)
            for way in range(2):
                scatter(g, way, 3, part).wait_recv()
            dq = (dq_all[g, 0, at, :] + rs_in[g, 0, 3, at, :].astype(F32)
                  + rs_in[g, 1, 3, at, :].astype(F32))
            dq_done[g, at, :] = (dq * SCALE).astype(BF16)
        for j in range(group):
            dq_store(g, j).start()

    def kv_send_off(g):
        for which, acc in ((0, dk_acc), (1, dv_acc)):
            kv_out[g, which] = acc[g, pre:2 * pre].astype(BF16)
            kv_grad(g, which).start()

    order = [(0, 4), (0, 5), (0, 3), (0, 6), (0, 2), (1, 4), (0, 7), (0, 1), (1, 5), (1, 3),
             (0, 0), (1, 6), (1, 2), (1, 7), (1, 1), (1, 0)]
    before = {0: [lambda: stats(0)], 5: [lambda: stats(1)]}
    after = {
        0: [lambda: scatter_first(0)],
        5: [lambda: scatter_first(1), lambda: scatter_next(0, 1)],
        10: [lambda: kv_send_off(0)],
        11: [lambda: scatter_next(1, 1), lambda: scatter_next(0, 2)],
        15: [lambda: kv_send_off(1)],
    }

    def grad_tick(e, _):
        for at, calls in before.items():
            @pl.when(e == at)
            def _():
                for call in calls:
                    call()

        g = jnp.int32(0)
        s = jnp.int32(0)
        for i, (a, b) in enumerate(order):
            g = jnp.where(e == i, a, g)
            s = jnp.where(e == i, b, s)
        second_pass(g, s)

        for at, calls in after.items():
            @pl.when(e == at)
            def _():
                for call in calls:
                    call()
        return 0

    lax.fori_loop(0, len(order), grad_tick, 0)

    for i in range(len(t1_codes)):
        t1_copy(i).wait()
    t_mid[1] = t_mid[0] + sum(t_in1[i] for i in range(len(t1_codes)))
    for i in range(len(t2_codes)):
        t2_copy(i).start()

    scatter_next(1, 2)
    scatter_next(0, 3)
    kv_finish(0)
    scatter_next(1, 3)
    scatter_last(0)
    kv_finish(1)

    for g in range(kv):
        for way in range(2):
            for part in range(2):
                for step in range(1, 5):
                    if step < 4 or part == way:
                        gather(g, way, step, part).wait_send()
                for step in range(4):
                    if step > 0 or part == way:
                        scatter(g, way, step, part).wait_send()
        for which in range(2):
            kv_grad(g, which).wait_send()

    for i in range(len(t2_codes)):
        t2_copy(i).wait()
    total = t_mid[1] + sum(t_in2[i] for i in range(len(t2_codes)))
    total = jnp.sum(total, axis=1, keepdims=True)
    place = lax.broadcasted_iota(jnp.int32, (levels, levels), 0)
    across = lax.broadcasted_iota(jnp.int32, (levels, levels), 1)
    dt_ref[...] = jnp.sum(
        jnp.where(place == across, total, 0.0), axis=0, keepdims=True)

    scatter_last(1)
    for g in range(kv):
        for which in range(2):
            kv_store(g, which).wait()
        for j in range(group):
            dq_store(g, j).wait()


def shards(queries, keys, values, grad_out, counts, rate_table, rate_index):
    n_head, n_req = lax.axis_size("head"), lax.axis_size("req")
    cand, pre = queries.shape[1], keys.shape[1]
    kv = keys.shape[2] // HD
    group = queries.shape[2] // keys.shape[2]
    levels = rate_table.shape[0]
    rows = group * cand
    lanes = rows // HD
    first = Z * min(n_req, 2) - 1
    second = n_head * 2 * (n_req // min(n_req, 2)) - 1
    any_ = pl.BlockSpec(memory_space=pl.ANY)
    smem = pl.BlockSpec(memory_space=pltpu.SMEM)
    vmem = pl.BlockSpec(memory_space=pltpu.VMEM)
    dma = pltpu.SemaphoreType.DMA
    out = pl.pallas_call(
        functools.partial(kernel, n_head, n_req, cand, pre, group, kv, levels),
        out_shape=(
            jax.ShapeDtypeStruct(queries.shape, BF16),
            jax.ShapeDtypeStruct(keys.shape, BF16),
            jax.ShapeDtypeStruct(values.shape, BF16),
            jax.ShapeDtypeStruct((1, levels), F32),
        ),
        in_specs=[smem, smem, vmem, any_, any_, any_, any_],
        out_specs=(any_, any_, any_, vmem),
        scratch_shapes=[
            pltpu.VMEM((Z, kv, 2, rows, HD), BF16),
            pltpu.VMEM((kv, 2 * pre, HD), BF16),
            pltpu.VMEM((kv, 2 * pre, HD), BF16),
            pltpu.VMEM((kv, HD, 2 * pre), BF16),
            pltpu.VMEM((1, pre), jnp.int32),
            pltpu.VMEM((2 * pre, HD), F32),
            pltpu.VMEM((levels, 2 * pre), BF16),
            pltpu.VMEM((kv, Z, 2 * pre, rows), F32),
            pltpu.VMEM((kv, Z, 2 * pre, rows), F32),
            pltpu.VMEM((kv, Z, 1, rows), F32),
            pltpu.VMEM((kv, Z, 1, rows), F32),
            pltpu.VMEM((kv, Z, 2, rows), F32),
            pltpu.VMEM((kv, Z, levels, rows), F32),
            pltpu.VMEM((kv, Z, levels, rows), F32),
            pltpu.VMEM((kv, Z, 2 * lanes, HD), F32),
            pltpu.VMEM((kv, Z, 2 * lanes, HD), F32),
            pltpu.VMEM((kv, Z, 2, 2 * lanes, HD), F32),
            pltpu.VMEM((kv, Z, rows, HD), F32),
            pltpu.VMEM((kv, 2, 4, rows, HD), BF16),
            pltpu.VMEM((kv, 2, 4, rows, HD), BF16),
            pltpu.VMEM((kv, rows, HD), BF16),
            pltpu.VMEM((kv, 2 * pre, HD), F32),
            pltpu.VMEM((kv, 2 * pre, HD), F32),
            pltpu.VMEM((kv, 2, pre, HD), BF16),
            pltpu.VMEM((kv, 2, pre, HD), BF16),
            pltpu.VMEM((kv, 2, pre, HD), BF16),
            pltpu.VMEM((2, levels, HD), F32),
            pltpu.VMEM((first, levels, HD), F32),
            pltpu.VMEM((second, levels, HD), F32),
            dma((kv * (2 * group + 2),)),
            dma((kv, 2 + group)),
            dma((kv, 2)),
            dma((kv, 2)),
            dma,
            dma,
            dma((kv, 2, 2, 4)),
            dma((kv, 2, 2, 4)),
            dma((kv, Z)),
            dma((kv, Z)),
            dma((kv, Z)),
            dma((kv, Z)),
            dma((kv, 2, 4, 2)),
            dma((kv, 2, 4, 2)),
            dma((kv, 2)),
            dma((kv, 2)),
            dma((first,)),
            dma((first,)),
            dma((second,)),
            dma((second,)),
        ],
        compiler_params=pltpu.CompilerParams(
            collective_id=0, has_side_effects=True, vmem_limit_bytes=60 * 1024 * 1024),
    )(counts, rate_table, rate_index, queries, keys, values, grad_out)
    return out[0], out[1], out[2], out[3].reshape(levels)


def solution(mesh):
    split = P("req", "ctx", "head")
    return jax.shard_map(
        shards,
        mesh=mesh,
        in_specs=(split, split, split, split, P("req"), P(), P("req", "ctx")),
        out_specs=(split, split, split, P()),
        check_vma=False,
    )
```

time: 94.5 us -> 67.7 us (0.72)
  the two profiles are of different devices: /device:TPU:1 before, /device:TPU:8 now
where the time goes in v2:
time: 67.7 us; the launch traced here: 67.5 us
  Pallas kernels  62.4 us (92%)
  local copies, waits for them, and re-layouts  3.73 us (6%)
  between operations  1.3 us (2%)
    pallas_call x1, Pallas kernels, shards(): pl.pallas_call(functools.partial(kernel, n_head, n_req, cand, pre, group,...  62.4 us
    unnamed x10, local copies, waits for them, and re-layouts  3.73 us

profile of v2, /device:TPU:8, one launch (start us, length us, event | category | flops | bytes accessed | tf_op | source)
XLA Modules:
  0.0 67.5 jit_solution(6711928844670782488)
XLA Ops:
  1.3 62.4 %shard_map.102 = (bf16[1,64,1024]{2,1,0:T(8,128)(2,1)}, bf16[1,256,256]{2,1,0:T(8,128)(2,1)}, bf16[1,256,256]{2,1,0:T(8,128)(2,1)}, f32[1,16]{1,0:T(1,128)}) custom-call(s32[1]{0:T(128)S(6)} %copy.15.counts_ref, f32[16]{0:T(128)} %table_ref.1, s32[1,256]{1,0:T(1,128)} %index_ref.1, bf16[1,64,1024]{2,1,0:T(8,128)(2,1)} %q_hbm.1, bf16[1,256,256]{2,1,0:T(8,128)(2,1)} %k_hbm.1, ...), custom_call_target="tpu_custom_call" | custom-call | tf_op jit(solution)/shard_map/pallas_call | solution.py:447
  63.7 0.0 copy-start.1
  63.7 1.6 %copy.16 = bf16[1,64,1024]{2,1,0:T(8,128)(2,1)} copy(bf16[1,64,1024]{2,1,0:T(8,128)(2,1)} %get-tuple-element.16) | data formatting | bytes 262144
  65.3 0.0 copy-done.1
  65.3 0.0 copy-start
  65.3 0.7 copy.17
  66.0 0.3 copy-done
  66.3 0.0 copy-start.2
  66.3 0.7 copy.18
  67.0 0.0 copy-done.2
  67.0 0.5 copy.19
Async XLA Ops:
  63.7 1.6 %copy-start.1 = (bf16[1,256,256]{2,1,0:T(8,128)(2,1)S(1)}, bf16[1,256,256]{2,1,0:T(8,128)(2,1)}, u32[]{:S(2)}) copy-start(bf16[1,256,256]{2,1,0:T(8,128)(2,1)} %get-tuple-element.17) | copy-start | bytes 393220
  65.3 1.0 %copy-start = (bf16[1,256,256]{2,1,0:T(8,128)(2,1)S(1)}, bf16[1,256,256]{2,1,0:T(8,128)(2,1)}, u32[]{:S(2)}) copy-start(bf16[1,256,256]{2,1,0:T(8,128)(2,1)} %get-tuple-element.18) | copy-start | bytes 393220
  66.3 0.7 copy-start.2

commit v3 on v2

--- a/solution.py
+++ b/solution.py
@@ -17,6 +17,8 @@
 NT = (((1,), (1,)), ((), ()))
 TN = (((0,), (0,)), ((), ()))
 NN = (((1,), (0,)), ((), ()))
+NEAR = (6, 2, 7, 1)
+FAR = (4, 5, 3)
 
 
 def kernel(
@@ -26,11 +28,11 @@
     qo, ks, vs, kt, idx_par, bias, onehot,
     probs, dprobs, peaks, deltas, fin, lev_a, lev_b, st_loc, st_in, st_all,
     dq_all, rs_out, rs_in, dq_done, dk_acc, dv_acc, kv_out, kv_in, kv_done,
-    t_mid, t_in1, t_in2,
+    t_mid, t_in1, t_in2, t_in3,
     in_sem, out_sem, kv_send, kv_recv, ix_send, ix_recv,
     ag_send, ag_recv, sa_send, sa_recv, sb_send, sb_recv,
     rs_send, rs_recv, dk_send, dk_recv,
-    t1_send, t1_recv, t2_send, t2_recv,
+    t1_send, t1_recv, t2_send, t2_recv, t3_send, t3_recv,
 ):
     rows = group * cand
     half = rows // 2
@@ -50,22 +52,20 @@
 
     partner = {"ctx": (1 - y) * Z + z}
     right, left = along_z(1), along_z(Z - 1)
-    t1_codes = [(a, b) for a in range(Z) for b in range(n_core)][1:]
-    t2_codes = [
-        (a, b, c) for a in range(n_head) for b in range(2) for c in range(n_hi)][1:]
-
-    def t1_peer(a, b):
-        return {"ctx": y * Z + (z + a) % Z, "req": hi * n_core + (core + b) % n_core}
-
-    def t2_peer(a, b, c):
+    far_right, far_left = along_z(2), along_z(Z - 2)
+    t2_codes = [(a, b) for a in range(n_head) for b in range(n_core)][1:]
+    t3_codes = [(a, b) for a in range(2) for b in range(n_hi)][1:]
+
+    def t2_peer(a, b):
+        return {"head": (head + a) % n_head, "req": hi * n_core + (core + b) % n_core}
+
+    def t3_peer(a, b):
         return {
-            "head": (head + a) % n_head,
-            "ctx": ((y + b) % 2) * Z + z,
-            "req": ((hi + c) % n_hi) * n_core + core,
-        }
+            "ctx": ((y + a) % 2) * Z + z, "req": ((hi + b) % n_hi) * n_core + core}
 
     barrier = pltpu.get_barrier_semaphore()
-    peers = [t1_peer(*code) for code in t1_codes] + [t2_peer(*code) for code in t2_codes]
+    peers = [left, right]
+    peers += [t2_peer(*code) for code in t2_codes] + [t3_peer(*code) for code in t3_codes]
     for peer in peers:
         pl.semaphore_signal(barrier, inc=1, device_id=peer, device_id_type=MESH)
 
@@ -87,7 +87,6 @@
     for copy in loads + late_loads:
         copy.start()
 
-    rs_in[:, :, 0] = jnp.zeros_like(rs_in[:, :, 0])
     dk_acc[...] = jnp.zeros_like(dk_acc)
     dv_acc[...] = jnp.zeros_like(dv_acc)
 
@@ -152,20 +151,24 @@
         return remote(
             rs_out.at[g, way, step, at, :], rs_in.at[g, way, step, at, :],
             rs_send.at[g, way, step, part], rs_recv.at[g, way, step, part],
-            (left, right)[way])
+            (far_left, far_right)[way] if step == 0 else (left, right)[way])
 
     def kv_grad(g, which):
         return remote(
             kv_out.at[g, which], kv_in.at[g, which],
             dk_send.at[g, which], dk_recv.at[g, which], partner)
 
-    def t1_copy(i):
-        return remote(
-            t_mid.at[0], t_in1.at[i], t1_send.at[i], t1_recv.at[i], t1_peer(*t1_codes[i]))
+    def t1_copy(o):
+        return remote(
+            t_mid.at[0], t_in1.at[o], t1_send.at[o], t1_recv.at[o], along_z(o))
 
     def t2_copy(i):
         return remote(
             t_mid.at[1], t_in2.at[i], t2_send.at[i], t2_recv.at[i], t2_peer(*t2_codes[i]))
+
+    def t3_copy(i):
+        return remote(
+            t_mid.at[2], t_in3.at[i], t3_send.at[i], t3_recv.at[i], t3_peer(*t3_codes[i]))
 
     for g in range(kv):
         for part in range(2):
@@ -175,9 +178,6 @@
             ix_copy.start()
         for which in range(2):
             kv_copy(g, which).start()
-
-    ix_copy.wait()
-    offsets(idx_par[...], 1)
 
     def split(row):
         return [row[:, i * HD:(i + 1) * HD] for i in range(lanes)]
@@ -216,13 +216,13 @@
         return total, delta
 
     def combine(g):
-        total, delta = merged([st_loc[g, 0]] + [st_in[g, o] for o in range(1, Z) if o != 4])
+        total, delta = merged([st_loc[g, 0]] + [st_in[g, o] for o in NEAR])
         st_all[g, 0, 0] = jnp.concatenate([total, delta], axis=0)
 
     def finish(g):
         def one(s, acc):
-            total, delta = merged([
-                st_all[g, lax.rem(Z - s, Z), 0], st_all[g, lax.rem(12 - s, Z), 1]])
+            total, delta = merged([st_all[g, lax.rem(Z - s, Z), 0]] + [
+                st_all[g, lax.rem(Z + o - s, Z), 1 + i] for i, o in enumerate(FAR)])
             delta = joined(delta)
             factor = jnp.exp2(peaks[g, s] - joined(total))
             fin[g, s] = jnp.concatenate([factor, delta], axis=0)
@@ -263,16 +263,9 @@
             out_sem.at[g, 2 + j])
 
     def gather_tick(t, _):
-        k, g = t // kv, t % kv
-
-        for i in range(kv):
-            @pl.when((k == 0) & (g == i))
-            def _():
-                for which in range(2):
-                    kv_copy(i, which).wait()
-                kt[i] = ks[i].astype(F32).T.astype(BF16)
-
-        @pl.when((k >= 1) & (k < 4))
+        k, g = 1 + t // kv, t % kv
+
+        @pl.when(k < 4)
         def _():
             for part in range(2):
                 for way in range(2):
@@ -284,41 +277,71 @@
 
         @pl.when(k == 4)
         def _():
+            for o in NEAR:
+                stat_a(g, o).wait()
+            combine(g)
             gather(g, 0, 4, 0).wait_recv()
             gather(g, 1, 4, 1).wait_recv()
 
+        for i in range(kv):
+            @pl.when((k == 1) & (g == i))
+            def _():
+                if i == 0:
+                    ix_copy.wait()
+                    offsets(idx_par[...], 1)
+                for which in range(2):
+                    kv_copy(i, which).wait()
+                kt[i] = ks[i].astype(F32).T.astype(BF16)
+
         def chunk(c, _):
-            first_pass(g, jnp.where(c == 0, (Z - k) % Z, k))
+            first_pass(g, jnp.where(c == 0, Z - k, jnp.where(c == 1, k, 0)))
             return 0
 
-        lax.fori_loop(0, jnp.where((k == 0) | (k == 4), 1, 2), chunk, 0)
-
-        @pl.when(k == 3)
+        lax.fori_loop(0, jnp.where(k == 4, 1, jnp.where(k == 1, 3, 2)), chunk, 0)
+
+        @pl.when(k == 2)
         def _():
-            for o in (5, 3, 6, 2, 7, 1):
+            for o in NEAR:
                 stat_a(g, o).start()
 
         @pl.when(k == 4)
         def _():
-            for o in (5, 3, 6, 2, 7, 1):
-                stat_a(g, o).wait()
-            combine(g)
-            st_all[g, 0, 1] = st_loc[g, 4]
+            for i, o in enumerate(FAR):
+                st_all[g, 0, 1 + i] = st_loc[g, o]
             for o in (4, 5, 3, 6, 2, 7, 1):
                 stat_b(g, o).start()
 
         return 0
 
-    lax.fori_loop(0, 5 * kv, gather_tick, 0)
+    lax.fori_loop(0, 4 * kv, gather_tick, 0)
 
     def stats(g):
         for o in (1, 7, 2, 6, 3, 5, 4):
             stat_b(g, o).wait()
         term = finish(g)
+        place = lax.broadcasted_iota(jnp.int32, (levels, HD), 0)
+        across = lax.broadcasted_iota(jnp.int32, (levels, HD), 1)
+        term = jnp.sum(term, axis=1, keepdims=True)
+        term = jnp.sum(jnp.where(place == across, term, 0.0), axis=0, keepdims=True)
         t_mid[0] = term if g == 0 else t_mid[0] + term
-        if g == kv - 1:
-            for i in range(len(t1_codes)):
-                t1_copy(i).start()
+
+    def table_first():
+        for o in range(1, Z):
+            t1_copy(o).start()
+
+    def table_second():
+        for o in range(1, Z):
+            t1_copy(o).wait()
+        t_mid[1] = t_mid[0] + sum(t_in1[o] for o in range(1, Z))
+        for i in range(len(t2_codes)):
+            t2_copy(i).start()
+
+    def table_third():
+        for i in range(len(t2_codes)):
+            t2_copy(i).wait()
+        t_mid[2] = t_mid[1] + sum(t_in2[i] for i in range(len(t2_codes)))
+        for i in range(len(t3_codes)):
+            t3_copy(i).start()
 
     def scatter_first(g):
         for way in range(2):
@@ -330,12 +353,14 @@
         for part in range(2):
             for way in range(2):
                 at = pl.ds(part * half, half)
-                if step > 1 or part == way:
+                dq = dq_all[g, 4 + step if way == 0 else 4 - step, at, :]
+                if step == 2 and part == way:
+                    scatter(g, way, 0, part).wait_recv()
+                    dq = dq + rs_in[g, way, 0, at, :].astype(F32)
+                if step > 1:
                     scatter(g, way, step - 1, part).wait_recv()
-                s = 4 + step if way == 0 else 4 - step
-                rs_out[g, way, step, at, :] = (
-                    dq_all[g, s, at, :] + rs_in[g, way, step - 1, at, :].astype(F32)
-                ).astype(BF16)
+                    dq = dq + rs_in[g, way, step - 1, at, :].astype(F32)
+                rs_out[g, way, step, at, :] = dq.astype(BF16)
                 scatter(g, way, step, part).start()
 
     def scatter_last(g):
@@ -354,15 +379,17 @@
             kv_out[g, which] = acc[g, pre:2 * pre].astype(BF16)
             kv_grad(g, which).start()
 
-    order = [(0, 4), (0, 5), (0, 3), (0, 6), (0, 2), (1, 4), (0, 7), (0, 1), (1, 5), (1, 3),
-             (0, 0), (1, 6), (1, 2), (1, 7), (1, 1), (1, 0)]
-    before = {0: [lambda: stats(0)], 5: [lambda: stats(1)]}
+    order = [(0, 4), (0, 5), (0, 3), (1, 4), (1, 5), (1, 3), (0, 6), (0, 2), (1, 6), (1, 2),
+             (0, 7), (0, 1), (0, 0), (1, 7), (1, 1), (1, 0)]
+    before = {0: [lambda: stats(0)], 3: [lambda: stats(1), table_first]}
     after = {
         0: [lambda: scatter_first(0)],
-        5: [lambda: scatter_first(1), lambda: scatter_next(0, 1)],
-        10: [lambda: kv_send_off(0)],
-        11: [lambda: scatter_next(1, 1), lambda: scatter_next(0, 2)],
-        15: [lambda: kv_send_off(1)],
+        2: [lambda: scatter_next(0, 1)],
+        3: [lambda: scatter_first(1)],
+        5: [lambda: scatter_next(1, 1)],
+        9: [lambda: scatter_next(0, 2), table_second],
+        12: [lambda: scatter_next(1, 2), lambda: kv_send_off(0)],
+        15: [lambda: kv_send_off(1), table_third],
     }
 
     def grad_tick(e, _):
@@ -388,18 +415,10 @@
 
     lax.fori_loop(0, len(order), grad_tick, 0)
 
-    for i in range(len(t1_codes)):
-        t1_copy(i).wait()
-    t_mid[1] = t_mid[0] + sum(t_in1[i] for i in range(len(t1_codes)))
-    for i in range(len(t2_codes)):
-        t2_copy(i).start()
-
-    scatter_next(1, 2)
     scatter_next(0, 3)
+    scatter_next(1, 3)
     kv_finish(0)
-    scatter_next(1, 3)
     scatter_last(0)
-    kv_finish(1)
 
     for g in range(kv):
         for way in range(2):
@@ -413,21 +432,33 @@
         for which in range(2):
             kv_grad(g, which).wait_send()
 
-    for i in range(len(t2_codes)):
-        t2_copy(i).wait()
-    total = t_mid[1] + sum(t_in2[i] for i in range(len(t2_codes)))
-    total = jnp.sum(total, axis=1, keepdims=True)
-    place = lax.broadcasted_iota(jnp.int32, (levels, levels), 0)
-    across = lax.broadcasted_iota(jnp.int32, (levels, levels), 1)
-    dt_ref[...] = jnp.sum(
-        jnp.where(place == across, total, 0.0), axis=0, keepdims=True)
-
+    kv_finish(1)
     scatter_last(1)
+    for i in range(len(t3_codes)):
+        t3_copy(i).wait()
+    total = t_mid[2] + sum(t_in3[i] for i in range(len(t3_codes)))
+    dt_ref[...] = total[:, 0:levels]
+
     for g in range(kv):
         for which in range(2):
             kv_store(g, which).wait()
         for j in range(group):
             dq_store(g, j).wait()
+
+
+def placed(*refs):
+    sources, results, stages, sem = refs[:4], refs[4:8], refs[8:12], refs[12]
+    fetch = [pltpu.make_async_copy(a, b, sem.at[0, i])
+             for i, (a, b) in enumerate(zip(sources, stages))]
+    store = [pltpu.make_async_copy(a, b, sem.at[1, i])
+             for i, (a, b) in enumerate(zip(stages, results))]
+    for copy in fetch:
+        copy.start()
+    for first, second in zip(fetch, store):
+        first.wait()
+        second.start()
+    for copy in store:
+        copy.wait()
 
 
 def shards(queries, keys, values, grad_out, counts, rate_table, rate_index):
@@ -438,8 +469,8 @@
     levels = rate_table.shape[0]
     rows = group * cand
     lanes = rows // HD
-    first = Z * min(n_req, 2) - 1
-    second = n_head * 2 * (n_req // min(n_req, 2)) - 1
+    second = max(n_head * min(n_req, 2) - 1, 1)
+    third = 2 * (n_req // min(n_req, 2)) - 1
     any_ = pl.BlockSpec(memory_space=pl.ANY)
     smem = pl.BlockSpec(memory_space=pltpu.SMEM)
     vmem = pl.BlockSpec(memory_space=pltpu.VMEM)
@@ -471,7 +502,7 @@
             pltpu.VMEM((kv, Z, levels, rows), F32),
             pltpu.VMEM((kv, Z, 2 * lanes, HD), F32),
             pltpu.VMEM((kv, Z, 2 * lanes, HD), F32),
-            pltpu.VMEM((kv, Z, 2, 2 * lanes, HD), F32),
+            pltpu.VMEM((kv, Z, 4, 2 * lanes, HD), F32),
             pltpu.VMEM((kv, Z, rows, HD), F32),
             pltpu.VMEM((kv, 2, 4, rows, HD), BF16),
             pltpu.VMEM((kv, 2, 4, rows, HD), BF16),
@@ -481,9 +512,10 @@
             pltpu.VMEM((kv, 2, pre, HD), BF16),
             pltpu.VMEM((kv, 2, pre, HD), BF16),
             pltpu.VMEM((kv, 2, pre, HD), BF16),
-            pltpu.VMEM((2, levels, HD), F32),
-            pltpu.VMEM((first, levels, HD), F32),
-            pltpu.VMEM((second, levels, HD), F32),
+            pltpu.VMEM((3, 1, HD), F32),
+            pltpu.VMEM((Z, 1, HD), F32),
+            pltpu.VMEM((second, 1, HD), F32),
+            pltpu.VMEM((third, 1, HD), F32),
             dma((kv * (2 * group + 2),)),
             dma((kv, 2 + group)),
             dma((kv, 2)),
@@ -500,14 +532,24 @@
             dma((kv, 2, 4, 2)),
             dma((kv, 2)),
             dma((kv, 2)),
-            dma((first,)),
-            dma((first,)),
+            dma((Z,)),
+            dma((Z,)),
             dma((second,)),
             dma((second,)),
+            dma((third,)),
+            dma((third,)),
         ],
         compiler_params=pltpu.CompilerParams(
             collective_id=0, has_side_effects=True, vmem_limit_bytes=60 * 1024 * 1024),
     )(counts, rate_table, rate_index, queries, keys, values, grad_out)
+    out = pl.pallas_call(
+        placed,
+        out_shape=tuple(jax.ShapeDtypeStruct(x.shape, x.dtype) for x in out),
+        in_specs=[any_] * 4,
+        out_specs=(any_,) * 4,
+        scratch_shapes=[pltpu.VMEM(x.shape, x.dtype) for x in out] + [dma((2, 4))],
+        compiler_params=pltpu.CompilerParams(vmem_limit_bytes=60 * 1024 * 1024),
+    )(*out)
     return out[0], out[1], out[2], out[3].reshape(levels)
 
 

time: 67.7 us -> 60.7 us (0.90)
  the two profiles are of different devices: /device:TPU:8 before, /device:TPU:1 now
where the time goes in v3:
time: 60.7 us; the launch traced here: 60.5 us
  Pallas kernels  59.2 us (98%)
  between operations  1.29 us (2%)
    pallas_call x1, Pallas kernels, shards(): pl.pallas_call(functools.partial(kernel, n_head, n_req, cand, pre, group,...  57.4 us
    pallas_call x1, Pallas kernels, shards(): pl.pallas_call(placed, out_shape=tuple((jax.ShapeDtypeStruct(x.shape, x.d...  1.76 us

profile of v3, /device:TPU:1, one launch (start us, length us, event | category | flops | bytes accessed | tf_op | source)
XLA Modules:
  0.0 60.5 jit_solution(2224634204611604827)
XLA Ops:
  1.3 57.4 %shard_map.102 = (bf16[1,64,1024]{2,1,0:T(8,128)(2,1)}, bf16[1,256,256]{2,1,0:T(8,128)(2,1)}, bf16[1,256,256]{2,1,0:T(8,128)(2,1)}, f32[1,16]{1,0:T(1,128)}) custom-call(s32[1]{0:T(128)S(6)} %copy.11.counts_ref, f32[16]{0:T(128)} %table_ref.1, s32[1,256]{1,0:T(1,128)} %index_ref.1, bf16[1,64,1024]{2,1,0:T(8,128)(2,1)} %q_hbm.1, bf16[1,256,256]{2,1,0:T(8,128)(2,1)} %k_hbm.1, ...), custom_call_target="tpu_custom_call" | custom-call | tf_op jit(solution)/shard_map/pallas_call | solution.py:478
  58.7 1.8 %shard_map.103 = (bf16[1,64,1024]{2,1,0:T(8,128)(2,1)}, bf16[1,256,256]{2,1,0:T(8,128)(2,1)}, bf16[1,256,256]{2,1,0:T(8,128)(2,1)}, f32[1,16]{1,0:T(1,128)}) custom-call(bf16[1,64,1024]{2,1,0:T(8,128)(2,1)} %get-tuple-element.12.refs_0_, bf16[1,256,256]{2,1,0:T(8,128)(2,1)} %get-tuple-element.13.refs_1_, bf16[1,256,256]{2,1,0:T(8,128)(2,1)} %get-tuple-element.14.refs_2_, ...), custom_call_target="tpu_custom_call" | custom-call | tf_op jit(solution)/shard_map/pallas_call | solution.py:545

commit v4 on v3

--- a/solution.py
+++ b/solution.py
@@ -19,6 +19,7 @@
 NN = (((1,), (0,)), ((), ()))
 NEAR = (6, 2, 7, 1)
 FAR = (4, 5, 3)
+SHORT = (0, 1)
 
 
 def kernel(
@@ -151,7 +152,7 @@
         return remote(
             rs_out.at[g, way, step, at, :], rs_in.at[g, way, step, at, :],
             rs_send.at[g, way, step, part], rs_recv.at[g, way, step, part],
-            (far_left, far_right)[way] if step == 0 else (left, right)[way])
+            (far_left, far_right)[way] if step == 0 and g in SHORT else (left, right)[way])
 
     def kv_grad(g, which):
         return remote(
@@ -220,16 +221,16 @@
         st_all[g, 0, 0] = jnp.concatenate([total, delta], axis=0)
 
     def finish(g):
-        def one(s, acc):
-            total, delta = merged([st_all[g, lax.rem(Z - s, Z), 0]] + [
-                st_all[g, lax.rem(Z + o - s, Z), 1 + i] for i, o in enumerate(FAR)])
+        acc = []
+        for s in range(Z):
+            total, delta = merged([st_all[g, (Z - s) % Z, 0]] + [
+                st_all[g, (Z + o - s) % Z, 1 + i] for i, o in enumerate(FAR)])
             delta = joined(delta)
             factor = jnp.exp2(peaks[g, s] - joined(total))
             fin[g, s] = jnp.concatenate([factor, delta], axis=0)
             term = factor * (lev_a[g, s] - (delta - deltas[g, s]) * lev_b[g, s])
-            return acc + functools.reduce(lambda a, b: a + b, split(term))
-
-        return lax.fori_loop(0, Z, one, jnp.zeros((levels, HD), F32))
+            acc += split(term)
+        return sum(acc)
 
     def second_pass(g, s):
         both = fin[g, s]
@@ -354,7 +355,7 @@
             for way in range(2):
                 at = pl.ds(part * half, half)
                 dq = dq_all[g, 4 + step if way == 0 else 4 - step, at, :]
-                if step == 2 and part == way:
+                if step == (2 if g in SHORT else 1) and part == way:
                     scatter(g, way, 0, part).wait_recv()
                     dq = dq + rs_in[g, way, 0, at, :].astype(F32)
                 if step > 1:
@@ -387,9 +388,10 @@
         2: [lambda: scatter_next(0, 1)],
         3: [lambda: scatter_first(1)],
         5: [lambda: scatter_next(1, 1)],
-        9: [lambda: scatter_next(0, 2), table_second],
-        12: [lambda: scatter_next(1, 2), lambda: kv_send_off(0)],
-        15: [lambda: kv_send_off(1), table_third],
+        11: [lambda: scatter_next(0, 2)],
+        12: [lambda: kv_send_off(0)],
+        14: [lambda: scatter_next(1, 2), table_second],
+        15: [lambda: kv_send_off(1)],
     }
 
     def grad_tick(e, _):
@@ -417,6 +419,7 @@
 
     scatter_next(0, 3)
     scatter_next(1, 3)
+    table_third()
     kv_finish(0)
     scatter_last(0)
 

time: 60.7 us -> 58.2 us (0.959)
  Pallas kernels: 59.2 us -> 56.7 us
    pallas_call x1, Pallas kernels: 57.4 us -> 54.9 us  [shards(): pl.pallas_call(functools.partial(kernel, n_head, n_req, cand, pre, group,...]
where the time goes in v4:
time: 58.2 us; the launch traced here: 58 us
  Pallas kernels  56.7 us (97%)
  between operations  1.29 us (2%)
    pallas_call x1, Pallas kernels, shards(): pl.pallas_call(functools.partial(kernel, n_head, n_req, cand, pre, group,...  54.9 us
    pallas_call x1, Pallas kernels, shards(): pl.pallas_call(placed, out_shape=tuple((jax.ShapeDtypeStruct(x.shape, x.d...  1.76 us

profile of v4, /device:TPU:1, one launch (start us, length us, event | category | flops | bytes accessed | tf_op | source)
XLA Modules:
  0.0 58.0 jit_solution(14412116255529343748)
XLA Ops:
  1.3 54.9 %shard_map.102 = (bf16[1,64,1024]{2,1,0:T(8,128)(2,1)}, bf16[1,256,256]{2,1,0:T(8,128)(2,1)}, bf16[1,256,256]{2,1,0:T(8,128)(2,1)}, f32[1,16]{1,0:T(1,128)}) custom-call(s32[1]{0:T(128)S(6)} %copy.11.counts_ref, f32[16]{0:T(128)} %table_ref.1, s32[1,256]{1,0:T(1,128)} %index_ref.1, bf16[1,64,1024]{2,1,0:T(8,128)(2,1)} %q_hbm.1, bf16[1,256,256]{2,1,0:T(8,128)(2,1)} %k_hbm.1, ...), custom_call_target="tpu_custom_call" | custom-call | tf_op jit(solution)/shard_map/pallas_call | solution.py:481
  56.2 1.8 %shard_map.103 = (bf16[1,64,1024]{2,1,0:T(8,128)(2,1)}, bf16[1,256,256]{2,1,0:T(8,128)(2,1)}, bf16[1,256,256]{2,1,0:T(8,128)(2,1)}, f32[1,16]{1,0:T(1,128)}) custom-call(bf16[1,64,1024]{2,1,0:T(8,128)(2,1)} %get-tuple-element.12.refs_0_, bf16[1,256,256]{2,1,0:T(8,128)(2,1)} %get-tuple-element.13.refs_1_, bf16[1,256,256]{2,1,0:T(8,128)(2,1)} %get-tuple-element.14.refs_2_, ...), custom_call_target="tpu_custom_call" | custom-call | tf_op jit(solution)/shard_map/pallas_call | solution.py:548

commit v5 on v4

--- a/solution.py
+++ b/solution.py
@@ -450,17 +450,11 @@
 
 
 def placed(*refs):
-    sources, results, stages, sem = refs[:4], refs[4:8], refs[8:12], refs[12]
-    fetch = [pltpu.make_async_copy(a, b, sem.at[0, i])
-             for i, (a, b) in enumerate(zip(sources, stages))]
-    store = [pltpu.make_async_copy(a, b, sem.at[1, i])
-             for i, (a, b) in enumerate(zip(stages, results))]
-    for copy in fetch:
+    copies = [
+        pltpu.make_async_copy(refs[i], refs[4 + i], refs[8].at[i]) for i in range(4)]
+    for copy in copies:
         copy.start()
-    for first, second in zip(fetch, store):
-        first.wait()
-        second.start()
-    for copy in store:
+    for copy in copies:
         copy.wait()
 
 
@@ -543,15 +537,15 @@
             dma((third,)),
         ],
         compiler_params=pltpu.CompilerParams(
-            collective_id=0, has_side_effects=True, vmem_limit_bytes=60 * 1024 * 1024),
+            collective_id=0, has_side_effects=True, vmem_limit_bytes=54784 * 1024),
     )(counts, rate_table, rate_index, queries, keys, values, grad_out)
     out = pl.pallas_call(
         placed,
         out_shape=tuple(jax.ShapeDtypeStruct(x.shape, x.dtype) for x in out),
         in_specs=[any_] * 4,
         out_specs=(any_,) * 4,
-        scratch_shapes=[pltpu.VMEM(x.shape, x.dtype) for x in out] + [dma((2, 4))],
-        compiler_params=pltpu.CompilerParams(vmem_limit_bytes=60 * 1024 * 1024),
+        scratch_shapes=[dma((4,))],
+        compiler_params=pltpu.CompilerParams(vmem_limit_bytes=16 * 1024 * 1024),
     )(*out)
     return out[0], out[1], out[2], out[3].reshape(levels)
 

time: 58.2 us -> 56.5 us (0.971)
  Pallas kernels: 56.7 us -> 55 us
    pallas_call x1, Pallas kernels: 1.76 us -> 0.78 us  [shards(): pl.pallas_call(placed, out_shape=tuple((jax.ShapeDtypeStruct(x.shape, x.d...]
    pallas_call x1, Pallas kernels: 54.9 us -> 54.2 us  [shards(): pl.pallas_call(functools.partial(kernel, n_head, n_req, cand, pre, group,...]
where the time goes in v5:
time: 56.5 us; the launch traced here: 56.4 us
  Pallas kernels  55 us (97%)
  between operations  1.34 us (2%)
    pallas_call x1, Pallas kernels, shards(): pl.pallas_call(functools.partial(kernel, n_head, n_req, cand, pre, group,...  54.2 us

profile of v5, /device:TPU:1, one launch (start us, length us, event | category | flops | bytes accessed | tf_op | source)
XLA Modules:
  0.0 56.4 jit_solution(8322184504893290667)
XLA Ops:
  0.6 0.0 copy-start
  0.6 0.0 copy-start.1
  1.3 0.0 copy-done
  1.3 0.0 copy-done.1
  1.3 54.2 %shard_map.102 = (bf16[1,64,1024]{2,1,0:T(8,128)(2,1)S(1)}, bf16[1,256,256]{2,1,0:T(8,128)(2,1)S(1)}, bf16[1,256,256]{2,1,0:T(8,128)(2,1)S(1)}, f32[1,16]{1,0:T(1,128)S(1)}) custom-call(s32[1]{0:T(128)S(6)} %copy.11.counts_ref, f32[16]{0:T(128)S(1)} %copy-done.1, s32[1,256]{1,0:T(1,128)S(1)} %copy-done, bf16[1,64,1024]{2,1,0:T(8,128)(2,1)} %q_hbm.1, ...), custom_call_target="tpu_custom_call" | custom-call | tf_op jit(solution)/shard_map/pallas_call | solution.py:475
  55.6 0.8 %shard_map.103 = (bf16[1,64,1024]{2,1,0:T(8,128)(2,1)}, bf16[1,256,256]{2,1,0:T(8,128)(2,1)}, bf16[1,256,256]{2,1,0:T(8,128)(2,1)}, f32[1,16]{1,0:T(1,128)}) custom-call(bf16[1,64,1024]{2,1,0:T(8,128)(2,1)S(1)} %get-tuple-element.12.refs_0_, bf16[1,256,256]{2,1,0:T(8,128)(2,1)S(1)} %get-tuple-element.13.refs_1_, ...), custom_call_target="tpu_custom_call" | custom-call | tf_op jit(solution)/shard_map/pallas_call | solution.py:542
Async XLA Ops:
  0.6 0.7 %copy-start = (s32[1,256]{1,0:T(1,128)S(1)}, s32[1,256]{1,0:T(1,128)}, u32[]{:S(2)}) copy-start(s32[1,256]{1,0:T(1,128)} %index_ref.1) | copy-start | bytes 3076
  0.6 0.7 %copy-start.1 = (f32[16]{0:T(128)S(1)}, f32[16]{0:T(128)}, u32[]{:S(2)}) copy-start(f32[16]{0:T(128)} %table_ref.1) | copy-start | bytes 196

commit v6 on v5

--- a/solution.py
+++ b/solution.py
@@ -88,6 +88,81 @@
     for copy in loads + late_loads:
         copy.start()
 
+    pl.semaphore_wait(barrier, len(peers))
+
+    def remote(src, dst, send, recv, device):
+        return pltpu.make_async_remote_copy(
+            src_ref=src, dst_ref=dst, send_sem=send, recv_sem=recv,
+            device_id=device, device_id_type=MESH)
+
+    def gather(g, way, step, part):
+        if way == 0:
+            src, dst, device = lax.rem(9 - step, Z), Z - step, right
+        else:
+            src, dst, device = step - 1, step, left
+        return remote(
+            qo.at[src, g, part], qo.at[dst, g, part],
+            ag_send.at[g, way, part, step - 1], ag_recv.at[g, way, part, step - 1], device)
+
+    def kv_copy(g, which):
+        ref = (ks, vs)[which]
+        return remote(
+            ref.at[g, pl.ds(0, pre), :], ref.at[g, pl.ds(pre, pre), :],
+            kv_send.at[g, which], kv_recv.at[g, which], partner)
+
+    ix_copy = remote(index_ref, idx_par, ix_send, ix_recv, partner)
+
+    def stat_a(g, o):
+        return remote(
+            st_loc.at[g, o], st_in.at[g, o],
+            sa_send.at[g, o], sa_recv.at[g, o], along_z(o))
+
+    def stat_b(g, o):
+        return remote(
+            st_all.at[g, 0], st_all.at[g, o],
+            sb_send.at[g, o], sb_recv.at[g, o], along_z(o))
+
+    def scatter(g, way, step, part):
+        at = pl.ds(part * half, half)
+        return remote(
+            rs_out.at[g, way, step, at, :], rs_in.at[g, way, step, at, :],
+            rs_send.at[g, way, step, part], rs_recv.at[g, way, step, part],
+            (far_left, far_right)[way] if step == 0 and g in SHORT else (left, right)[way])
+
+    def kv_grad(g, which):
+        return remote(
+            kv_out.at[g, which], kv_in.at[g, which],
+            dk_send.at[g, which], dk_recv.at[g, which], partner)
+
+    def t1_copy(o):
+        return remote(
+            t_mid.at[0], t_in1.at[o], t1_send.at[o], t1_recv.at[o], along_z(o))
+
+    def t2_copy(i):
+        return remote(
+            t_mid.at[1], t_in2.at[i], t2_send.at[i], t2_recv.at[i], t2_peer(*t2_codes[i]))
+
+    def t3_copy(i):
+        return remote(
+            t_mid.at[2], t_in3.at[i], t3_send.at[i], t3_recv.at[i], t3_peer(*t3_codes[i]))
+
+    live = counts_ref[0] - ctx * cand
+    slot = lax.rem(lax.broadcasted_iota(jnp.int32, (rows, HD), 0), cand)
+    for g in range(kv):
+        for part in range(2):
+            for j in range(group):
+                loads[2 * (g * group + j) + part].wait()
+            if part == 1:
+                qo[0, g, 1] = jnp.where(
+                    slot < live, qo[0, g, 1], jnp.zeros((rows, HD), BF16))
+            for way in range(2):
+                gather(g, way, 1, part).start()
+    ix_copy.start()
+    for g in range(kv):
+        for which in range(2):
+            late_loads[2 * g + which].wait()
+            kv_copy(g, which).start()
+
     dk_acc[...] = jnp.zeros_like(dk_acc)
     dv_acc[...] = jnp.zeros_like(dv_acc)
 
@@ -105,80 +180,6 @@
             hot, table, TN, preferred_element_type=F32) * LOG2E
 
     offsets(index_ref[...], 0)
-
-    for copy in loads + late_loads:
-        copy.wait()
-    live = counts_ref[0] - ctx * cand
-    slot = lax.rem(lax.broadcasted_iota(jnp.int32, (rows, HD), 0), cand)
-    for g in range(kv):
-        qo[0, g, 1] = jnp.where(slot < live, qo[0, g, 1], jnp.zeros((rows, HD), BF16))
-
-    pl.semaphore_wait(barrier, len(peers))
-
-    def remote(src, dst, send, recv, device):
-        return pltpu.make_async_remote_copy(
-            src_ref=src, dst_ref=dst, send_sem=send, recv_sem=recv,
-            device_id=device, device_id_type=MESH)
-
-    def gather(g, way, step, part):
-        if way == 0:
-            src, dst, device = lax.rem(9 - step, Z), Z - step, right
-        else:
-            src, dst, device = step - 1, step, left
-        return remote(
-            qo.at[src, g, part], qo.at[dst, g, part],
-            ag_send.at[g, way, part, step - 1], ag_recv.at[g, way, part, step - 1], device)
-
-    def kv_copy(g, which):
-        ref = (ks, vs)[which]
-        return remote(
-            ref.at[g, pl.ds(0, pre), :], ref.at[g, pl.ds(pre, pre), :],
-            kv_send.at[g, which], kv_recv.at[g, which], partner)
-
-    ix_copy = remote(index_ref, idx_par, ix_send, ix_recv, partner)
-
-    def stat_a(g, o):
-        return remote(
-            st_loc.at[g, o], st_in.at[g, o],
-            sa_send.at[g, o], sa_recv.at[g, o], along_z(o))
-
-    def stat_b(g, o):
-        return remote(
-            st_all.at[g, 0], st_all.at[g, o],
-            sb_send.at[g, o], sb_recv.at[g, o], along_z(o))
-
-    def scatter(g, way, step, part):
-        at = pl.ds(part * half, half)
-        return remote(
-            rs_out.at[g, way, step, at, :], rs_in.at[g, way, step, at, :],
-            rs_send.at[g, way, step, part], rs_recv.at[g, way, step, part],
-            (far_left, far_right)[way] if step == 0 and g in SHORT else (left, right)[way])
-
-    def kv_grad(g, which):
-        return remote(
-            kv_out.at[g, which], kv_in.at[g, which],
-            dk_send.at[g, which], dk_recv.at[g, which], partner)
-
-    def t1_copy(o):
-        return remote(
-            t_mid.at[0], t_in1.at[o], t1_send.at[o], t1_recv.at[o], along_z(o))
-
-    def t2_copy(i):
-        return remote(
-            t_mid.at[1], t_in2.at[i], t2_send.at[i], t2_recv.at[i], t2_peer(*t2_codes[i]))
-
-    def t3_copy(i):
-        return remote(
-            t_mid.at[2], t_in3.at[i], t3_send.at[i], t3_recv.at[i], t3_peer(*t3_codes[i]))
-
-    for g in range(kv):
-        for part in range(2):
-            for way in range(2):
-                gather(g, way, 1, part).start()
-        if g == 0:
-            ix_copy.start()
-        for which in range(2):
-            kv_copy(g, which).start()
 
     def split(row):
         return [row[:, i * HD:(i + 1) * HD] for i in range(lanes)]

time: 56.5 us -> 56.5 us (level)
  no operation moved by 1% of the time
where the time goes in v6:
time: 56.5 us; the launch traced here: 56.4 us
  Pallas kernels  55 us (97%)
  between operations  1.34 us (2%)
    pallas_call x1, Pallas kernels, shards(): pl.pallas_call(functools.partial(kernel, n_head, n_req, cand, pre, group,...  54.2 us

profile of v6, /device:TPU:1, one launch (start us, length us, event | category | flops | bytes accessed | tf_op | source)
XLA Modules:
  0.0 56.4 jit_solution(572364347122470622)
XLA Ops:
  0.6 0.0 copy-start
  0.6 0.0 copy-start.1
  1.3 0.0 copy-done
  1.3 0.0 copy-done.1
  1.3 54.2 %shard_map.102 = (bf16[1,64,1024]{2,1,0:T(8,128)(2,1)S(1)}, bf16[1,256,256]{2,1,0:T(8,128)(2,1)S(1)}, bf16[1,256,256]{2,1,0:T(8,128)(2,1)S(1)}, f32[1,16]{1,0:T(1,128)S(1)}) custom-call(s32[1]{0:T(128)S(6)} %copy.11.counts_ref, f32[16]{0:T(128)S(1)} %copy-done.1, s32[1,256]{1,0:T(1,128)S(1)} %copy-done, bf16[1,64,1024]{2,1,0:T(8,128)(2,1)} %q_hbm.1, ...), custom_call_target="tpu_custom_call" | custom-call | tf_op jit(solution)/shard_map/pallas_call | solution.py:476
  55.6 0.8 %shard_map.103 = (bf16[1,64,1024]{2,1,0:T(8,128)(2,1)}, bf16[1,256,256]{2,1,0:T(8,128)(2,1)}, bf16[1,256,256]{2,1,0:T(8,128)(2,1)}, f32[1,16]{1,0:T(1,128)}) custom-call(bf16[1,64,1024]{2,1,0:T(8,128)(2,1)S(1)} %get-tuple-element.12.refs_0_, bf16[1,256,256]{2,1,0:T(8,128)(2,1)S(1)} %get-tuple-element.13.refs_1_, ...), custom_call_target="tpu_custom_call" | custom-call | tf_op jit(solution)/shard_map/pallas_call | solution.py:543
Async XLA Ops:
  0.6 0.7 %copy-start = (s32[1,256]{1,0:T(1,128)S(1)}, s32[1,256]{1,0:T(1,128)}, u32[]{:S(2)}) copy-start(s32[1,256]{1,0:T(1,128)} %index_ref.1) | copy-start | bytes 3076
  0.6 0.7 %copy-start.1 = (f32[16]{0:T(128)S(1)}, f32[16]{0:T(128)}, u32[]{:S(2)}) copy-start(f32[16]{0:T(128)} %table_ref.1) | copy-start | bytes 196

commit v7 on v6

--- a/solution.py
+++ b/solution.py
@@ -123,7 +123,7 @@
             sb_send.at[g, o], sb_recv.at[g, o], along_z(o))
 
     def scatter(g, way, step, part):
-        at = pl.ds(part * half, half)
+        at = pl.ds(part * half, half) if step == 0 else pl.ds(0, rows)
         return remote(
             rs_out.at[g, way, step, at, :], rs_in.at[g, way, step, at, :],
             rs_send.at[g, way, step, part], rs_recv.at[g, way, step, part],
@@ -352,27 +352,25 @@
             scatter(g, way, 0, way).start()
 
     def scatter_next(g, step):
-        for part in range(2):
-            for way in range(2):
-                at = pl.ds(part * half, half)
+        for way in range(2):
+            dq = dq_all[g, 4 + step if way == 0 else 4 - step]
+            if step > 1:
+                scatter(g, way, step - 1, 0).wait_recv()
+                dq = dq + rs_in[g, way, step - 1].astype(F32)
+            rs_out[g, way, step] = dq.astype(BF16)
+            if step == 2:
+                scatter(g, way, 0, way).wait_recv()
+                at = pl.ds(way * half, half)
                 dq = dq_all[g, 4 + step if way == 0 else 4 - step, at, :]
-                if step == (2 if g in SHORT else 1) and part == way:
-                    scatter(g, way, 0, part).wait_recv()
-                    dq = dq + rs_in[g, way, 0, at, :].astype(F32)
-                if step > 1:
-                    scatter(g, way, step - 1, part).wait_recv()
-                    dq = dq + rs_in[g, way, step - 1, at, :].astype(F32)
+                dq = dq + rs_in[g, way, 1, at, :].astype(F32) + rs_in[g, way, 0, at, :].astype(F32)
                 rs_out[g, way, step, at, :] = dq.astype(BF16)
-                scatter(g, way, step, part).start()
+            scatter(g, way, step, 0).start()
 
     def scatter_last(g):
-        for part in range(2):
-            at = pl.ds(part * half, half)
-            for way in range(2):
-                scatter(g, way, 3, part).wait_recv()
-            dq = (dq_all[g, 0, at, :] + rs_in[g, 0, 3, at, :].astype(F32)
-                  + rs_in[g, 1, 3, at, :].astype(F32))
-            dq_done[g, at, :] = (dq * SCALE).astype(BF16)
+        for way in range(2):
+            scatter(g, way, 3, 0).wait_recv()
+        dq = dq_all[g, 0] + rs_in[g, 0, 3].astype(F32) + rs_in[g, 1, 3].astype(F32)
+        dq_done[g] = (dq * SCALE).astype(BF16)
         for j in range(group):
             dq_store(g, j).start()
 
@@ -431,7 +429,7 @@
                     if step < 4 or part == way:
                         gather(g, way, step, part).wait_send()
                 for step in range(4):
-                    if step > 0 or part == way:
+                    if part == (0 if step > 0 else way):
                         scatter(g, way, step, part).wait_send()
         for which in range(2):
             kv_grad(g, which).wait_send()

time: 56.5 us -> 56.5 us (level)
  no operation moved by 1% of the time
where the time goes in v7:
time: 56.5 us
  Pallas kernels  55.1 us (98%)
  between operations  1.34 us (2%)
    pallas_call x1, Pallas kernels, shards(): pl.pallas_call(functools.partial(kernel, n_head, n_req, cand, pre, group,...  54.3 us

profile of v7, /device:TPU:1, one launch (start us, length us, event | category | flops | bytes accessed | tf_op | source)
XLA Modules:
  0.0 56.5 jit_solution(8350857753071450284)
XLA Ops:
  0.6 0.0 copy-start
  0.6 0.0 copy-start.1
  1.3 0.0 copy-done
  1.3 0.0 copy-done.1
  1.3 54.3 %shard_map.102 = (bf16[1,64,1024]{2,1,0:T(8,128)(2,1)S(1)}, bf16[1,256,256]{2,1,0:T(8,128)(2,1)S(1)}, bf16[1,256,256]{2,1,0:T(8,128)(2,1)S(1)}, f32[1,16]{1,0:T(1,128)S(1)}) custom-call(s32[1]{0:T(128)S(6)} %copy.11.counts_ref, f32[16]{0:T(128)S(1)} %copy-done.1, s32[1,256]{1,0:T(1,128)S(1)} %copy-done, bf16[1,64,1024]{2,1,0:T(8,128)(2,1)} %q_hbm.1, ...), custom_call_target="tpu_custom_call" | custom-call | tf_op jit(solution)/shard_map/pallas_call | solution.py:474
  55.7 0.8 %shard_map.103 = (bf16[1,64,1024]{2,1,0:T(8,128)(2,1)}, bf16[1,256,256]{2,1,0:T(8,128)(2,1)}, bf16[1,256,256]{2,1,0:T(8,128)(2,1)}, f32[1,16]{1,0:T(1,128)}) custom-call(bf16[1,64,1024]{2,1,0:T(8,128)(2,1)S(1)} %get-tuple-element.12.refs_0_, bf16[1,256,256]{2,1,0:T(8,128)(2,1)S(1)} %get-tuple-element.13.refs_1_, ...), custom_call_target="tpu_custom_call" | custom-call | tf_op jit(solution)/shard_map/pallas_call | solution.py:541
Async XLA Ops:
  0.6 0.7 %copy-start = (s32[1,256]{1,0:T(1,128)S(1)}, s32[1,256]{1,0:T(1,128)}, u32[]{:S(2)}) copy-start(s32[1,256]{1,0:T(1,128)} %index_ref.1) | copy-start | bytes 3076
  0.6 0.7 %copy-start.1 = (f32[16]{0:T(128)S(1)}, f32[16]{0:T(128)}, u32[]{:S(2)}) copy-start(f32[16]{0:T(128)} %table_ref.1) | copy-start | bytes 196
